TPU v7x, 256 devices: a whole 4x4x8 slice. The times are simulated.
256 devices in a mesh: seg: 16 (over y, x_lo, core), samp: 2 (over x_hi), dp: 8 (over z).
Axes of the slice: x: 4 (x_hi: 2, x_lo: 2; x = x_hi * 2 + x_lo), y: 4, z: 8, core: 2. Of those that a mesh axis runs over, the one named last changes fastest.
Arguments:
- head_start: bfloat16 [16384, 8192], P('dp', ('seg', 'samp')), may hold values from -6 to 6
- flow_start: bfloat16 [16384, 8192], P('dp', ('seg', 'samp')), may hold values from -4 to 4
- impedance: float32 [16384, 8], P('dp'), may hold values from 0.5 to 2
- friction: float32 [16384, 8], P('dp'), may hold values from 0.05 to 0.5
- seg_count: int32 [16384], P('dp'), may hold values from 1 to 8
- junction_code: int32 [16384, 8], P('dp'), may hold values from 0 to 2
- boundary_code: int32 [16384], P('dp'), may hold values from 0 to 2
- head_up: float32 [16384], P('dp'), may hold values from 0.5 to 2
- head_down: float32 [16384], P('dp'), may hold values from -1 to 1
- opening: float32 [16384], P('dp'), may hold values from 0.2 to 2
- window_start: int32 [16384], P('dp'), may hold values from 0 to 4096
- layer_weights: bfloat16 [2, 1024, 1024], replicated, may hold values from -0.1875 to 0.1875
Outputs:
- head_end: bfloat16 [16384, 8192], P('dp', ('seg', 'samp'))
- weight_grads: float32 [2, 1024, 1024], P(None, ('seg', 'samp', 'dp'))
Inputs may be any that keep to these rules, and one draw needn't show every extreme that they name: Each pipe is cut into seg_count equal sections. `boundary_code`: 0 reservoir, 1 closed end, 2 valve.
All inputs are finite; a program needn't handle non-finite values.
Results may differ from a plain program's by a relative error of at most 0.0004.
The roundings to bfloat16 on the way count: a program that leaves them out, or rounds other values in their place, can miss the bound.
Values may be sent and summed in bfloat16 or wider, within the bound.
A program may use at most 128 MiB of HBM per device.

v0:
```python
import jax
import jax.numpy as jnp
from jax import lax
from jax.sharding import PartitionSpec as P


def padded_2(block, sides, width):
    for axis, dim in sides:
        count = lax.axis_size(axis)
        forward = [(i, i + 1) for i in range(count - 1)]
        backward = [(target, source) for source, target in forward]
        low = lax.ppermute(
            lax.slice_in_dim(block, block.shape[dim] - width, None, axis=dim), axis, forward
        )
        high = lax.ppermute(lax.slice_in_dim(block, 0, width, axis=dim), axis, backward)
        block = jnp.concatenate([low, block, high], axis=dim)
    return block


def section_fields(glob_cells, seg_total, impedance, friction, junction, cell_total):
    placed = jnp.clip(glob_cells, 0, cell_total - 1)
    section = placed[None, :] * seg_total[:, None] // cell_total
    wave = jnp.zeros(section.shape, jnp.float32)
    damping = jnp.zeros(section.shape, jnp.float32)
    for section_id in range(impedance.shape[1]):
        picked = section == section_id
        wave = jnp.where(picked, impedance[:, section_id : section_id + 1], wave)
        damping = jnp.where(
            picked,
            friction[:, section_id : section_id + 1]
            * (1.0 + junction[:, section_id : section_id + 1].astype(jnp.float32)),
            damping,
        )
    return (wave, damping)


def characteristic_step(heads, flows, wave, damping, glob_inner, params, cell_total):
    upper_head, lower_head, valve_open, boundary = params
    left_head = heads[:, :-2]
    left_flow = flows[:, :-2]
    right_head = heads[:, 2:]
    right_flow = flows[:, 2:]
    forward_char = left_head + wave * left_flow - damping * left_flow * jnp.abs(left_flow)
    backward_char = right_head - wave * right_flow + damping * right_flow * jnp.abs(right_flow)
    new_head = 0.5 * (forward_char + backward_char)
    new_flow = (forward_char - backward_char) / (2.0 * wave)
    at_start = (glob_inner == 0)[None, :]
    at_finish = (glob_inner == cell_total - 1)[None, :]
    valve_head = forward_char / (1.0 + wave * valve_open)
    end_head = jnp.where(
        boundary == 0, lower_head, jnp.where(boundary == 1, forward_char, valve_head)
    )
    end_flow = jnp.where(
        boundary == 0,
        (forward_char - lower_head) / wave,
        jnp.where(boundary == 1, jnp.zeros_like(forward_char), valve_open * valve_head),
    )
    new_head = jnp.where(at_start, upper_head, jnp.where(at_finish, end_head, new_head))
    new_flow = jnp.where(
        at_start, (upper_head - backward_char) / wave, jnp.where(at_finish, end_flow, new_flow)
    )
    return (new_head, new_flow)


def body(
    head_start,
    flow_start,
    impedance,
    friction,
    seg_count,
    junction_code,
    boundary_code,
    head_up,
    head_down,
    opening,
    window_start,
    layer_weights,
):
    group_size = lax.axis_size(("seg", "samp"))
    cell_dev = head_start.shape[1]
    cell_total = cell_dev * group_size
    offset = lax.axis_index(("seg", "samp")) * cell_dev
    params = (head_up[:, None], head_down[:, None], opening[:, None], boundary_code[:, None])
    state = jnp.stack([head_start.astype(jnp.float32), flow_start.astype(jnp.float32)])
    glob_inner = offset + jnp.arange(cell_dev, dtype=jnp.int32)
    wave, damping = section_fields(
        glob_inner, seg_count, impedance, friction, junction_code, cell_total
    )
    heads = state[0]
    for step_number in range(2):
        padded = padded_2(state, ((("seg", "samp"), 2),), 1)
        heads, flows = characteristic_step(
            padded[0], padded[1], wave, damping, glob_inner, params, cell_total
        )
        state = jnp.stack([heads, flows])
    head_end = heads.astype(jnp.bfloat16)
    start_rows, end_rows = (
        lax.all_to_all(head_start, ("seg", "samp"), split_axis=0, concat_axis=1, tiled=True),
        lax.all_to_all(head_end, ("seg", "samp"), split_axis=0, concat_axis=1, tiled=True),
    )
    per_rows = start_rows.shape[0]
    width = layer_weights.shape[1]
    span = cell_total // 2
    starts = lax.dynamic_slice_in_dim(
        window_start, lax.axis_index(("seg", "samp")) * per_rows, per_rows
    )
    cutter = jax.vmap(lambda row_values, begin: lax.dynamic_slice_in_dim(row_values, begin, span))
    inputs = cutter(start_rows, starts).reshape(-1, width)
    targets = cutter(end_rows, starts).reshape(-1, width)
    row_total = window_start.shape[0] * lax.axis_size("dp") * (span // width)
    layers = layer_weights.shape[0]
    activations = [inputs]
    pre_values = []
    current = inputs
    output = None
    for layer_number in range(layers):
        product = jnp.dot(current, layer_weights[layer_number], preferred_element_type=jnp.float32)
        if layer_number + 1 < layers:
            pre_values.append(product)
            current = jax.nn.silu(product).astype(jnp.bfloat16)
            activations.append(current)
        else:
            output = product
    error = output - targets.astype(jnp.float32)
    grad_rows = (error * (8.0 / row_total)).astype(jnp.bfloat16)
    grads = [None] * layers
    for layer_number in reversed(range(layers)):
        grads[layer_number] = jnp.dot(
            activations[layer_number].T, grad_rows, preferred_element_type=jnp.float32
        )
        if layer_number > 0:
            back = jnp.dot(
                grad_rows, layer_weights[layer_number].T, preferred_element_type=jnp.float32
            )
            pre_value = pre_values[layer_number - 1]
            sigma = jax.nn.sigmoid(pre_value)
            grad_rows = (back * sigma * (1.0 + pre_value * (1.0 - sigma))).astype(jnp.bfloat16)
    stacked = jnp.stack(grads)
    summed = lax.psum_scatter(stacked, ("seg", "samp", "dp"), scatter_dimension=1, tiled=True)
    return (head_end, summed)


def solution(mesh):
    placed = (
        P("dp", ("seg", "samp")),
        P("dp", ("seg", "samp")),
        P("dp", None),
        P("dp", None),
        P("dp"),
        P("dp", None),
        P("dp"),
        P("dp"),
        P("dp"),
        P("dp"),
        P("dp"),
        P(),
    )
    return jax.shard_map(
        body,
        mesh=mesh,
        in_specs=placed,
        out_specs=(P("dp", ("seg", "samp")), P(None, ("seg", "samp", "dp"), None)),
        check_vma=False,
    )
```

profile of v0, /device:TPU:2, one launch (start us, length us, event | category | flops | bytes accessed | tf_op | source)
XLA Modules:
  0.0 751.1 jit_solution(4997231671312138899)
XLA Ops:
  9.0 2.4 fusion.54
  13.8 4.0 collective-permute-start
  20.5 9.0 %all-to-all-start = ((bf16[32,64,256]{2,1,0:T(8,128)(2,1)}), bf16[32,64,256]{2,1,0:T(8,128)(2,1)S(1)}, u32[]{:S(2)}, u32[]{:S(2)}) async-start(bf16[32,64,256]{2,1,0:T(8,128)(2,1)} %bitcast.87), calls=%async_computation | async-start | bytes 2097152 | tf_op jit(solution)/shard_map/all_to_all | solution.py:98
  33.2 5.0 pad_maximum_fusion.1
  39.0 8.6 %select_bitcast_fusion = f32[1,2048,256]{2,1,0:T(8,128)S(1)} fusion(f32[2048]{0:T(1024)S(1)} %copy-done.3, f32[2048]{0:T(1024)S(1)} %copy-done.4, f32[2048]{0:T(1024)S(1)} %copy-done.5, pred[2048]{0:T(1024)(128)(4,1)S(1)} %get-tuple-element.65, pred[2048]{0:T(1024)(128)(4,1)S(1)} %get-tuple-element.64, pred[256]{0:T(512)(128)(4,1)S(1)} %get-tuple-element.66, ...), kind=kLoop, calls=%fused_computation.48 | loop fusion | flops 35127296 | bytes 10655232 | tf_op jit(solution)/shard_map/stack | solution.py:95
  47.6 8.4 %select_bitcast_fusion.1 = f32[1,2048,256]{2,1,0:T(8,128)S(1)} fusion(f32[2048]{0:T(1024)S(1)} %copy-done.3, f32[2048]{0:T(1024)S(1)} %copy-done.4, f32[2048]{0:T(1024)S(1)} %copy-done.5, pred[2048]{0:T(1024)(128)(4,1)S(1)} %get-tuple-element.65, pred[2048]{0:T(1024)(128)(4,1)S(1)} %get-tuple-element.64, pred[256]{0:T(512)(128)(4,1)S(1)} %get-tuple-element.66, ...), kind=kLoop, calls=%fused_computation.49 | loop fusion | flops 31981568 | bytes 10655232 | tf_op jit(solution)/shard_map/stack | solution.py:95
  56.0 2.7 fusion.4
  60.9 4.0 collective-permute-start.2
  71.3 3.0 collective-permute-done.3
  76.2 5.1 pad_maximum_fusion.2
  81.8 9.6 %fusion.23 = bf16[2048,256]{1,0:T(8,128)(2,1)} fusion(f32[2048,258]{1,0:T(8,128)S(1)} %get-tuple-element.41, f32[2048,258]{1,0:T(8,128)S(1)} %get-tuple-element.40, f32[2048]{0:T(1024)S(1)} %copy-done.3, f32[2048]{0:T(1024)S(1)} %bitcast.135, f32[2048]{0:T(1024)S(1)} %bitcast.138, f32[2048]{0:T(1024)S(1)} %bitcast.120, f32[2048]{0:T(1024)S(1)} %bitcast.123, ...), kind=kLoop, calls=%fused_computation.55 | loop fusion | flops 31981568 | bytes 9606656 | tf_op jit(solution)/shard_map/convert_element_type | solution.py:96
  91.4 6.0 all-to-all-start.1
  98.5 202.8 %while.2 = (s32[]{:T(128)}, bf16[64,8192]{1,0:T(8,128)(2,1)}, s32[64,2]{0,1:T(2,128)S(1)}, bf16[64,4096]{1,0:T(8,128)(2,1)S(1)}, s32[]{:T(128)}, /*index=5*/s32[]{:T(128)}) while((s32[]{:T(128)}, bf16[64,8192]{1,0:T(8,128)(2,1)}, s32[64,2]{0,1:T(2,128)S(1)}, bf16[64,4096]{1,0:T(8,128)(2,1)S(1)}, s32[]{:T(128)}, /*index=5*/s32[]{:T(128)}) %tuple.67), condition=%wide.while_cond, body=%wide.while_body.sunk | while | flops 2 | bytes 32881 | solution.py:107
  99.2 2.3 dynamic-slice.15
  102.3 2.3 dynamic-slice.15
  105.5 2.3 dynamic-slice.15
  108.7 2.3 dynamic-slice.15
  111.8 2.3 dynamic-slice.15
  115.0 2.3 dynamic-slice.15
  118.2 2.3 dynamic-slice.15
  121.3 2.3 dynamic-slice.15
  124.5 2.3 dynamic-slice.15
  127.7 2.3 dynamic-slice.15
  130.8 2.3 dynamic-slice.15
  134.0 2.3 dynamic-slice.15
  137.2 2.3 dynamic-slice.15
  140.3 2.3 dynamic-slice.15
  143.5 2.3 dynamic-slice.15
  146.7 2.3 dynamic-slice.15
  149.9 2.3 dynamic-slice.15
  153.0 2.3 dynamic-slice.15
  156.2 2.3 dynamic-slice.15
  159.4 2.3 dynamic-slice.15
  168.9 2.3 dynamic-slice.15
  175.2 2.3 dynamic-slice.15
  178.4 2.3 dynamic-slice.15
  184.7 2.3 dynamic-slice.15
  187.9 2.3 dynamic-slice.15
  194.2 2.3 dynamic-slice.15
  200.6 2.3 dynamic-slice.15
  203.7 2.3 dynamic-slice.15
  210.1 2.3 dynamic-slice.15
  213.2 2.3 dynamic-slice.15
  219.6 2.3 dynamic-slice.15
  229.1 2.3 dynamic-slice.15
  235.4 2.3 dynamic-slice.15
  238.6 2.3 dynamic-slice.15
  244.9 2.3 dynamic-slice.15
  248.1 2.3 dynamic-slice.15
  254.4 2.3 dynamic-slice.15
  260.8 2.3 dynamic-slice.15
  263.9 2.3 dynamic-slice.15
  270.3 2.3 dynamic-slice.15
  273.4 2.3 dynamic-slice.15
  279.8 2.3 dynamic-slice.15
  289.3 2.3 dynamic-slice.15
  295.6 2.3 dynamic-slice.15
  298.8 2.3 dynamic-slice.15
  301.6 3.3 fusion.18
  305.1 141.5 %while.3 = (s32[]{:T(128)}, bf16[64,8192]{1,0:T(8,128)(2,1)S(1)}, s32[64,2]{0,1:T(2,128)S(1)}, bf16[64,4096]{1,0:T(8,128)(2,1)S(1)}, s32[]{:T(128)}, /*index=5*/s32[]{:T(128)}) while((s32[]{:T(128)}, bf16[64,8192]{1,0:T(8,128)(2,1)S(1)}, s32[64,2]{0,1:T(2,128)S(1)}, bf16[64,4096]{1,0:T(8,128)(2,1)S(1)}, s32[]{:T(128)}, /*index=5*/s32[]{:T(128)}) %tuple.68), condition=%wide.while_cond.1, body=%wide.while_body.1.sunk | while | flops 2 | bytes 32881 | solution.py:107
  446.9 2.7 fusion.41
  449.6 5.3 convolution_bitcast_fusion.1
  457.1 4.1 pad_maximum_fusion
  461.2 281.6 %all-reduce.3.cloned.1.call-done = f32[2,1024,1024]{2,1,0:T(8,128)} async-done(((f32[2,1024,1024]{2,1,0:T(8,128)}), f32[2,1024,1024]{2,1,0:T(8,128)}) %all-reduce.3.cloned.1.call-update) | async-done | bytes 8388624
  (527 shorter events, 267.3 us)
Async XLA Ops:
  9.0 2.6 copy-start
  13.8 16.7 %collective-permute-start = (f32[2,2048,1]{1,0,2:T(2,128)S(1)}, f32[2,2048,1]{1,0,2:T(2,128)S(1)}, u32[]{:S(2)}, u32[]{:S(2)}) collective-permute-start(f32[2,2048,1]{1,0,2:T(2,128)S(1)} %copy.34), channel_id=1, source_target_pairs={{0,8},{8,16},{16,24},{24,32},{32,40},{40,48},{48,56},{56,64},{64,7... | collective-permute-start | bytes 49160 | tf_op jit(solution)/shard_map/ppermute | solution.py:12
  17.9 11.7 %copy-start.9 = (f32[2048,8]{0,1:T(8,128)S(1)}, f32[2048,8]{0,1:T(8,128)}, u32[]{:S(2)}) copy-start(f32[2048,8]{0,1:T(8,128)} %param.14) | copy-start | bytes 196612
  17.9 11.7 %copy-start.10 = (s32[2048]{0:T(1024)S(1)}, s32[2048]{0:T(1024)}, u32[]{:S(2)}) copy-start(s32[2048]{0:T(1024)} %param.18) | copy-start | bytes 24580
  17.9 11.7 %copy-start.7 = (s32[2048,8]{0,1:T(8,128)S(1)}, s32[2048,8]{0,1:T(8,128)}, u32[]{:S(2)}) copy-start(s32[2048,8]{0,1:T(8,128)} %param.17) | copy-start | bytes 196612
  17.9 11.7 %copy-start.8 = (f32[2048,8]{0,1:T(8,128)S(1)}, f32[2048,8]{0,1:T(8,128)}, u32[]{:S(2)}) copy-start(f32[2048,8]{0,1:T(8,128)} %param.15) | copy-start | bytes 196612
  18.5 12.7 %collective-permute-start.1 = (f32[2,2048,1]{1,0,2:T(2,128)S(1)}, f32[2,2048,1]{1,0,2:T(2,128)S(1)}, u32[]{:S(2)}, u32[]{:S(2)}) collective-permute-start(f32[2,2048,1]{1,0,2:T(2,128)S(1)} %copy.35), channel_id=1, source_target_pairs={{8,0},{16,8},{24,16},{32,24},{40,32},{48,40},{56,48},{64,56},{72,6... | collective-permute-start | bytes 49160 | tf_op jit(solution)/shard_map/ppermute | solution.py:15
  20.5 70.9 %all-to-all-start = ((bf16[32,64,256]{2,1,0:T(8,128)(2,1)}), bf16[32,64,256]{2,1,0:T(8,128)(2,1)S(1)}, u32[]{:S(2)}, u32[]{:S(2)}) async-start(bf16[32,64,256]{2,1,0:T(8,128)(2,1)} %bitcast.87), calls=%async_computation | async-start | bytes 2097152 | tf_op jit(solution)/shard_map/all_to_all | solution.py:98
  38.3 0.7 copy-start.3
  38.3 0.7 copy-start.4
  38.3 0.7 copy-start.5
  38.3 0.7 copy-start.6
  56.0 2.7 copy-start.1
  60.9 8.3 %collective-permute-start.2 = (f32[2,2048,1]{1,0,2:T(2,128)S(1)}, f32[2,2048,1]{1,0,2:T(2,128)S(1)}, u32[]{:S(2)}, u32[]{:S(2)}) collective-permute-start(f32[2,2048,1]{1,0,2:T(2,128)S(1)} %copy.38), channel_id=1, source_target_pairs={{0,8},{8,16},{16,24},{24,32},{32,40},{40,48},{48,56},{56,64},{64,7... | collective-permute-start | bytes 49160 | tf_op jit(solution)/shard_map/ppermute | solution.py:12
  67.1 7.1 collective-permute-start.3
  91.4 213.6 %all-to-all-start.1 = ((bf16[32,64,256]{2,1,0:T(8,128)(2,1)}), bf16[32,64,256]{2,1,0:T(8,128)(2,1)S(1)}, u32[]{:S(2)}, u32[]{:S(2)}) async-start(bf16[32,64,256]{2,1,0:T(8,128)(2,1)} %bitcast.29), calls=%async_computation.1 | async-start | bytes 2097152 | tf_op jit(solution)/shard_map/all_to_all | solution.py:99
  97.3 645.4 %all-reduce.3.cloned.1.call-start = ((), (), s32[]{:S(2)}) async-start(), calls=%async_computation.2 | async-start | bytes 16777216
  449.6 5.3 copy-start.11
  454.9 2.2 copy-start.2
Sparse Core Ops, SparseCore 0:
  461.3 281.4 all-reduce.2
where the time goes:
time: 757 us; the launch traced here: 751 us
  local copies, waits for them, and re-layouts  363 us (48%)
  waiting for transfers between devices  285 us (38%)
  other arithmetic  46.3 us (6%)
  starting transfers between devices  27.1 us (4%)
  between operations  14.4 us (2%)
  matrix products  12.1 us (2%)
    gather x512, local copies, waits for them, and re-layouts  341 us
    unnamed x2, waiting for transfers between devices  282 us
    another operation x3, other arithmetic, body(): state = jnp.stack([heads, flows])  19.7 us
  transfers between devices with their start and end apart: 7, of which 2 were waited for; matrix products, arithmetic and copies ran while one was open for 34% of the time, Pallas kernels for 0%

commit v1 on v0

v1 whole, which is shorter than its diff:
```python
import functools
import jax
import jax.numpy as jnp
from jax import lax
from jax.experimental import pallas as pl
from jax.experimental.pallas import tpu as pltpu
from jax.sharding import PartitionSpec as P

MESH = pl.DeviceIdType.MESH
GROUP = ("seg", "samp")
PLANE = 32
CELLS = 8192
BF16 = jnp.bfloat16
F32 = jnp.float32


def dot(lhs, rhs, lhs_dim, rhs_dim):
    return lax.dot_general(
        lhs, rhs, (((lhs_dim,), (rhs_dim,)), ((), ())), preferred_element_type=F32
    )


def pack_kernel(head_ref, flow_ref, out_ref):
    row = lax.broadcasted_iota(jnp.int32, (16, 256), 0)
    lane = lax.broadcasted_iota(jnp.int32, (16, 256), 1)
    wanted = jnp.where(row < 2, row, row + 252)
    pick = jnp.where((row < 4) & (lane == wanted), 1.0, 0.0).astype(BF16)
    heads = dot(pick, head_ref[...], 1, 1)
    flows = dot(pick, flow_ref[...], 1, 1)
    out_ref[0:2] = heads[0:2].astype(BF16)
    out_ref[2:4] = flows[0:2].astype(BF16)
    out_ref[4:6] = heads[2:4].astype(BF16)
    out_ref[6:8] = flows[2:4].astype(BF16)


def pack_edges(head, flow):
    return pl.pallas_call(
        pack_kernel, out_shape=jax.ShapeDtypeStruct((8, head.shape[0]), BF16)
    )(head, flow)


def stencil_kernel(table_ref, head_ref, flow_ref, halo_ref, out_ref, edge):
    rows = head_ref.shape[0]
    position = lax.axis_index(GROUP)
    first = position * 256
    row = lax.broadcasted_iota(jnp.int32, (8, 256), 0)
    lane2 = lax.broadcasted_iota(jnp.int32, (8, 256), 1)
    wanted = jnp.where(row < 4, (row % 2), 126 + (row % 2)) + jnp.where((row % 4) < 2, 0, 128)
    place = jnp.where(lane2 == wanted, 1.0, 0.0).astype(BF16)
    edge[...] = dot(halo_ref[...], place, 0, 0)
    step = 16
    lane = lax.broadcasted_iota(jnp.int32, (step, 384), 1)
    cell = jnp.where(lane < 320, lane, lane - 384) + first
    placed = jnp.clip(cell, 0, CELLS - 1)
    at_start = cell == 0
    at_finish = cell == CELLS - 1

    def run(is_edge, chunk, carry):
        here = pl.ds(pl.multiple_of(chunk * step, step), step)
        table = table_ref[here, :]
        count = table[:, 24:25].astype(jnp.int32)
        section = lax.shift_right_logical(placed * count, 13)

        def look(base):
            return jnp.concatenate(
                [
                    jnp.take_along_axis(table, section[:, c * 128 : c * 128 + 128] + base, axis=1)
                    for c in range(3)
                ],
                axis=1,
            )

        wave = look(0)
        loss = look(8)
        half = look(16)
        ends = edge[here, :]
        heads = jnp.concatenate([head_ref[here, :].astype(F32), ends[:, :128]], axis=1)
        flows = jnp.concatenate([flow_ref[here, :].astype(F32), ends[:, 128:]], axis=1)
        upper = table[:, 25:26]
        lower = table[:, 26:27]
        valve = table[:, 27:28]
        kind = table[:, 28:29]
        for number in range(2):
            lh = pltpu.roll(heads, 1, 1)
            lq = pltpu.roll(flows, 1, 1)
            rh = pltpu.roll(heads, 383, 1)
            rq = pltpu.roll(flows, 383, 1)
            if number == 1:
                lh, lq, rh, rq = (v[:, :256] for v in (lh, lq, rh, rq))
                wave, loss, half = (v[:, :256] for v in (wave, loss, half))
            forward = lh + wave * lq - loss * lq * jnp.abs(lq)
            backward = rh - wave * rq + loss * rq * jnp.abs(rq)
            width = forward.shape[1]
            new_heads = 0.5 * (forward + backward)
            if number == 0:
                new_flows = (forward - backward) * half
            if is_edge:
                start, finish = at_start[:, :width], at_finish[:, :width]
                valve_head = forward / (1.0 + wave * valve)
                end_head = jnp.where(kind == 0.0, lower, jnp.where(kind == 1.0, forward, valve_head))
                new_heads = jnp.where(start, upper, jnp.where(finish, end_head, new_heads))
                if number == 0:
                    end_flow = jnp.where(
                        kind == 0.0,
                        (forward - lower) * (2.0 * half),
                        jnp.where(kind == 1.0, 0.0, valve * valve_head),
                    )
                    new_flows = jnp.where(
                        start,
                        (upper - backward) * (2.0 * half),
                        jnp.where(finish, end_flow, new_flows),
                    )
            if number == 0:
                heads, flows = new_heads, new_flows
        out_ref[here, :] = new_heads.astype(BF16)
        return carry

    inner = (position > 0) & (position < PLANE - 1)

    @pl.when(inner)
    def _():
        lax.fori_loop(0, rows // step, functools.partial(run, False), 0, unroll=2)

    @pl.when(jnp.logical_not(inner))
    def _():
        lax.fori_loop(0, rows // step, functools.partial(run, True), 0)


def stencil(table, head, flow, halo):
    total = head.shape[0]
    rows = 256
    return pl.pallas_call(
        stencil_kernel,
        grid=(total // rows,),
        in_specs=[
            pl.BlockSpec((rows, 128), lambda i: (i, 0)),
            pl.BlockSpec((rows, 256), lambda i: (i, 0)),
            pl.BlockSpec((rows, 256), lambda i: (i, 0)),
            pl.BlockSpec((8, rows), lambda i: (0, i)),
        ],
        out_specs=pl.BlockSpec((rows, 256), lambda i: (i, 0)),
        out_shape=jax.ShapeDtypeStruct(head.shape, BF16),
        scratch_shapes=[pltpu.VMEM((rows, 256), F32)],
        cost_estimate=pl.CostEstimate(
            flops=total * 256 * 60, bytes_accessed=4 << 20, transcendentals=0
        ),
    )(table, head, flow, halo)


def cut_windows(rows_ref, begin_ref, out_ref):
    def group(number, carry):
        here = pl.ds(pl.multiple_of(number * 16, 16), 16)
        begin = begin_ref[here, :]
        block = lax.shift_right_logical(begin, 7)
        rest = begin & 127
        lane = lax.broadcasted_iota(jnp.int32, (16, 128), 1)
        values = []
        for source in range(PLANE):
            pair = rows_ref[source, here, :].astype(F32)
            values += [pair[:, :128], pair[:, 128:]]
        for bit, count in ((32, 64), (16, 48), (8, 40), (4, 36), (2, 34), (1, 33)):
            on = (block & bit) != 0
            values = [
                jnp.where(on, values[j + bit], values[j]) if j + bit < len(values) else values[j]
                for j in range(count)
            ]
        index = (lane + rest) & 127
        keep = lane + rest < 128
        turned = [jnp.take_along_axis(v, index, axis=1) for v in values]
        for j in range(32):
            piece = jnp.where(keep, turned[j], turned[j + 1]).astype(BF16)
            at = pl.ds(pl.multiple_of((j // 8) * 64 + number * 16, 16), 16)
            out_ref[at, (j % 8) * 128 : (j % 8) * 128 + 128] = piece
        return carry

    lax.fori_loop(0, 4, group, 0)


def forward_kernel(rows_ref, begin_ref, weights_ref, a0_ref, a1_ref, z_ref, out_ref):
    cut_windows(rows_ref, begin_ref, a0_ref)
    z = dot(a0_ref[...], weights_ref[0], 1, 0)
    z_ref[...] = z
    a1 = (z * jax.nn.sigmoid(z)).astype(BF16)
    a1_ref[...] = a1
    out_ref[...] = dot(a1, weights_ref[1], 1, 0)


def forward(rows, begin, weights):
    return pl.pallas_call(
        forward_kernel,
        out_shape=[
            jax.ShapeDtypeStruct((256, 1024), BF16),
            jax.ShapeDtypeStruct((256, 1024), BF16),
            jax.ShapeDtypeStruct((256, 1024), F32),
            jax.ShapeDtypeStruct((256, 1024), F32),
        ],
        compiler_params=pltpu.CompilerParams(vmem_limit_bytes=48 << 20),
        cost_estimate=pl.CostEstimate(
            flops=4 * 256 * 1024 * 1024, bytes_accessed=8 << 20, transcendentals=0
        ),
    )(rows, begin, weights)


def backward_kernel(scale, rows_ref, begin_ref, weights_ref, a0_ref, a1_ref, z_ref, output_ref, grads_ref, targets):
    cut_windows(rows_ref, begin_ref, targets)
    g1 = ((output_ref[...] - targets[...].astype(F32)) * scale).astype(BF16)
    grads_ref[1] = dot(a1_ref[...], g1, 0, 0)
    back = dot(g1, weights_ref[1], 1, 1)
    z = z_ref[...]
    sigma = jax.nn.sigmoid(z)
    g0 = (back * sigma * (1.0 + z * (1.0 - sigma))).astype(BF16)
    grads_ref[0] = dot(a0_ref[...], g0, 0, 0)


def backward(rows, begin, weights, a0, a1, z, output, scale):
    return pl.pallas_call(
        functools.partial(backward_kernel, scale),
        out_shape=jax.ShapeDtypeStruct((2, 1024, 1024), F32),
        scratch_shapes=[pltpu.VMEM((256, 1024), BF16)],
        compiler_params=pltpu.CompilerParams(vmem_limit_bytes=48 << 20),
        cost_estimate=pl.CostEstimate(
            flops=6 * 256 * 1024 * 1024, bytes_accessed=16 << 20, transcendentals=0
        ),
    )(rows, begin, weights, a0, a1, z, output)


def reduce_kernel(p_ref, out_ref, mine, other, a_in, b_in, a_sum, b_sum, a2_in, b2_in, z_sum, z_in, send, recv):
    seg, samp, z = lax.axis_index("seg"), lax.axis_index("samp"), lax.axis_index("dp")
    y, xlo, core = seg // 4, (seg // 2) % 2, seg % 2
    x = samp * 2 + xlo

    def at_x(t):
        return {"seg": y * 4 + (t % 2) * 2 + core, "samp": t // 2}

    def at_y(t):
        return {"seg": t * 4 + xlo * 2 + core}

    def at_z(t):
        return {"dp": t}

    at_core = {"seg": y * 4 + xlo * 2 + 1 - core}

    barrier = pltpu.get_barrier_semaphore()
    pl.semaphore_signal(barrier, inc=1, device_id=at_core, device_id_type=MESH)
    for p in range(1, 4):
        pl.semaphore_signal(barrier, inc=1, device_id=at_x((x + p) % 4), device_id_type=MESH)
        pl.semaphore_signal(barrier, inc=1, device_id=at_y((y + p) % 4), device_id_type=MESH)
    for p in range(1, 8):
        pl.semaphore_signal(barrier, inc=1, device_id=at_z((z + p) % 8), device_id_type=MESH)
    pl.semaphore_wait(barrier, 14)

    def copy(src, dst, number, device):
        return pltpu.make_async_remote_copy(
            src_ref=src,
            dst_ref=dst,
            send_sem=send.at[number],
            recv_sem=recv.at[number],
            device_id=device,
            device_id_type=MESH,
        )

    first = copy(p_ref.at[:, 1 - core], other, 0, at_core)
    first.start()
    first.wait()

    def add_core(i, c):
        mine[i] = p_ref[i, core] + other[i]
        return c

    lax.fori_loop(0, 16, add_core, 0)

    copies = []
    for p in range(1, 4):
        tx, ty = (x + p) % 4, (y + p) % 4
        for layer in range(2):
            for yy in range(4):
                k = 1 + ((p - 1) * 2 + layer) * 4 + yy
                copies.append(
                    copy(
                        mine.at[layer * 8 + yy * 2 + tx % 2, pl.ds(pl.multiple_of((tx // 2) * 32, 32), 32), pl.ds(0, 512)],
                        a_in.at[p - 1, layer * 4 + yy],
                        k,
                        at_x(tx),
                    )
                )
            for xx in range(2):
                k = 25 + ((p - 1) * 2 + layer) * 2 + xx
                copies.append(
                    copy(
                        mine.at[layer * 8 + ty * 2 + xx, :, pl.ds(512, 512)],
                        b_in.at[p - 1, layer * 2 + xx],
                        k,
                        at_y(ty),
                    )
                )
    for c in copies:
        c.start()
    for c in copies:
        c.wait()

    def add_a(i, c):
        own = mine[2 * i + xlo, pl.ds(pl.multiple_of(samp * 32, 32), 32), pl.ds(0, 512)]
        a_sum[i] = (own + a_in[0, i]) + (a_in[1, i] + a_in[2, i])
        return c

    lax.fori_loop(0, 8, add_a, 0)

    def add_b(i, c):
        own = mine[(i // 2) * 8 + y * 2 + i % 2, :, pl.ds(512, 512)]
        b_sum[i] = (own + b_in[0, i]) + (b_in[1, i] + b_in[2, i])
        return c

    lax.fori_loop(0, 4, add_b, 0)

    copies = []
    for p in range(1, 4):
        tx, ty = (x + p) % 4, (y + p) % 4
        for layer in range(2):
            k = 37 + (p - 1) * 2 + layer
            copies.append(copy(a_sum.at[layer * 4 + ty], a2_in.at[p - 1, layer], k, at_y(ty)))
            k = 43 + (p - 1) * 2 + layer
            copies.append(
                copy(
                    b_sum.at[layer * 2 + tx % 2, pl.ds(pl.multiple_of((tx // 2) * 32, 32), 32)],
                    b2_in.at[p - 1, layer],
                    k,
                    at_x(tx),
                )
            )
    for c in copies:
        c.start()
    for c in copies:
        c.wait()
    for layer in range(2):
        left = (a_sum[layer * 4 + y] + a2_in[0, layer]) + (a2_in[1, layer] + a2_in[2, layer])
        own = b_sum[layer * 2 + xlo, pl.ds(pl.multiple_of(samp * 32, 32), 32)]
        right = (own + b2_in[0, layer]) + (b2_in[1, layer] + b2_in[2, layer])
        for t in range(8):
            z_sum[t, 4 * layer : 4 * layer + 4, 0:512] = left[4 * t : 4 * t + 4]
            z_sum[t, 4 * layer : 4 * layer + 4, 512:1024] = right[4 * t : 4 * t + 4]
    copies = []
    for p in range(1, 8):
        t = (z + p) % 8
        copies.append(copy(z_sum.at[t], z_in.at[p - 1], 48 + p, at_z(t)))
    for c in copies:
        c.start()
    for c in copies:
        c.wait()
    total = z_sum[z]
    for p in range(7):
        total = total + z_in[p]
    out_ref[0] = total[0:4]
    out_ref[1] = total[4:8]


def reduce_scatter(grads):
    return pl.pallas_call(
        reduce_kernel,
        out_shape=jax.ShapeDtypeStruct((2, 4, 1024), F32),
        in_specs=[pl.BlockSpec(memory_space=pltpu.VMEM)],
        out_specs=pl.BlockSpec(memory_space=pltpu.VMEM),
        scratch_shapes=[
            pltpu.VMEM((16, 64, 1024), F32),
            pltpu.VMEM((16, 64, 1024), F32),
            pltpu.VMEM((3, 8, 32, 512), F32),
            pltpu.VMEM((3, 4, 64, 512), F32),
            pltpu.VMEM((8, 32, 512), F32),
            pltpu.VMEM((4, 64, 512), F32),
            pltpu.VMEM((3, 2, 32, 512), F32),
            pltpu.VMEM((3, 2, 32, 512), F32),
            pltpu.VMEM((8, 8, 1024), F32),
            pltpu.VMEM((7, 8, 1024), F32),
            pltpu.SemaphoreType.DMA((56,)),
            pltpu.SemaphoreType.DMA((56,)),
        ],
        compiler_params=pltpu.CompilerParams(
            collective_id=1, has_side_effects=True, vmem_limit_bytes=56 << 20
        ),
    )(grads.reshape(16, 2, 64, 1024))


def make_table(impedance, friction, seg_count, junction, boundary, head_up, head_down, opening):
    rows = impedance.shape[0]
    parts = [
        impedance,
        friction * (1.0 + junction.astype(F32)),
        0.5 / impedance,
        seg_count.astype(F32)[:, None],
        head_up[:, None],
        head_down[:, None],
        opening[:, None],
        boundary.astype(F32)[:, None],
        jnp.zeros((rows, 128 - 29), F32),
    ]
    return jnp.concatenate(parts, axis=1)


def spread(block):
    return lax.all_to_all(
        block.reshape(PLANE, 64, 256), GROUP, split_axis=0, concat_axis=0, tiled=True
    )


def body(
    head_start,
    flow_start,
    impedance,
    friction,
    seg_count,
    junction_code,
    boundary_code,
    head_up,
    head_down,
    opening,
    window_start,
    layer_weights,
):
    start_rows = spread(head_start)
    packed = pack_edges(head_start, flow_start)
    up = [(i, i + 1) for i in range(PLANE - 1)]
    down = [(i + 1, i) for i in range(PLANE - 1)]
    above = lax.ppermute(packed[:4], GROUP, down)
    below = lax.ppermute(packed[4:], GROUP, up)
    halo = jnp.concatenate([above, below], axis=0)
    table = make_table(
        impedance, friction, seg_count, junction_code, boundary_code, head_up, head_down, opening
    )
    head_end = stencil(table, head_start, flow_start, halo)
    end_rows = spread(head_end)
    begin = lax.dynamic_slice_in_dim(window_start, lax.axis_index(GROUP) * 64, 64)
    begin = jnp.broadcast_to(begin[:, None], (64, 128))
    a0, a1, z, output = forward(start_rows, begin, layer_weights)
    row_total = window_start.shape[0] * lax.axis_size("dp") * 4
    grads = backward(end_rows, begin, layer_weights, a0, a1, z, output, 8.0 / row_total)
    return (head_end, reduce_scatter(grads))


def solution(mesh):
    placed = (
        P("dp", ("seg", "samp")),
        P("dp", ("seg", "samp")),
        P("dp", None),
        P("dp", None),
        P("dp"),
        P("dp", None),
        P("dp"),
        P("dp"),
        P("dp"),
        P("dp"),
        P("dp"),
        P(),
    )
    return jax.shard_map(
        body,
        mesh=mesh,
        in_specs=placed,
        out_specs=(P("dp", ("seg", "samp")), P(None, ("seg", "samp", "dp"), None)),
        check_vma=False,
    )
```

time: 757 us -> 177 us (0.23)
  local copies, waits for them, and re-layouts: 363 us -> 26.8 us
  waiting for transfers between devices: 285 us -> 7.8 us
  Pallas kernels: 0 us -> 101 us
  other arithmetic: 46.3 us -> 3.78 us
  between operations: 14.4 us -> 0.76 us
  matrix products: 12.1 us -> 0 us
    gather x512 -> x0, local copies, waits for them, and re-layouts: 341 us -> none
    unnamed x2 -> x0, waiting for transfers between devices: 282 us -> none
    pallas_call x0 -> x5, Pallas kernels: none -> 101 us  [the longest x1 60.2 us: reduce_scatter(): pl.pallas_call(reduce_kernel, out_shape=jax.ShapeDtypeStruct((2, 4, 1024)...]
    another operation x5 -> x0, other arithmetic: 25.5 us -> none  [the longest x3 19.7 us: body(): state = jnp.stack([heads, flows])]
    all_to_all x2, starting transfers between devices: 15 us -> 27.2 us  [spread(): lax.all_to_all(block.reshape(PLANE, 64, 256), GROUP, split_axis=0, concat...]
    dot_general x4 -> x0, matrix products: 12.1 us -> none  [the longest x2 6.11 us: body(): jnp.dot(activations[layer_number].T, grad_rows, preferred_element_type=jn...]
    concatenate x2 -> x1, other arithmetic: 10.2 us -> 0.64 us  [body(): halo = jnp.concatenate([above, below], axis=0)]
    slice x6 -> x1, local copies, waits for them, and re-layouts: 9.72 us -> 0.85 us  [body(): above = lax.ppermute(packed[:4], GROUP, down)]
  transfers between devices with their start and end apart: 7 -> 4, of which waited for: 2 -> 1; matrix products, arithmetic and copies ran while one was open for 34% -> 13% of each run, Pallas kernels for 0% -> 19%
where the time goes in v1:
time: 177 us; the launch traced here: 174 us
  Pallas kernels  101 us (57%)
  starting transfers between devices  34.6 us (20%)
  local copies, waits for them, and re-layouts  26.8 us (15%)
  waiting for transfers between devices  7.8 us (4%)
  other arithmetic  3.78 us (2%)
    pallas_call x1, Pallas kernels, reduce_scatter(): pl.pallas_call(reduce_kernel, out_shape=jax.ShapeDtypeStruct((2, 4, 1024)...  60.2 us
    all_to_all x2, starting transfers between devices, spread(): lax.all_to_all(block.reshape(PLANE, 64, 256), GROUP, split_axis=0, concat...  27.2 us
    pallas_call x1, Pallas kernels, stencil(): pl.pallas_call(stencil_kernel, grid=(total // rows,), in_specs=[pl.BlockS...  25.5 us
    unnamed x20, local copies, waits for them, and re-layouts  8.48 us
    pallas_call x1, Pallas kernels, backward(): pl.pallas_call(functools.partial(backward_kernel, scale), out_shape=jax.S...  8.06 us
    all_to_all x2, waiting for transfers between devices, spread(): lax.all_to_all(block.reshape(PLANE, 64, 256), GROUP, split_axis=0, concat...  7.79 us
    concatenate x1, local copies, waits for them, and re-layouts, make_table(): return jnp.concatenate(parts, axis=1)  7.11 us
    ppermute x1, starting transfers between devices, body(): below = lax.ppermute(packed[4:], GROUP, up)  4.22 us
  transfers between devices with their start and end apart: 4, of which 1 were waited for; matrix products, arithmetic and copies ran while one was open for 13% of the time, Pallas kernels for 19%

profile of v1, /device:TPU:2, one launch (start us, length us, event | category | flops | bytes accessed | tf_op | source)
XLA Modules:
  0.0 174.5 jit_solution(5225580476939843689)
XLA Ops:
  0.6 0.0 copy-start.6
  0.6 0.0 copy-start.7
  0.7 0.0 copy-start.8
  0.7 7.8 %all-to-all-start.1 = ((bf16[32,64,256]{2,1,0:T(8,128)(2,1)}), bf16[32,64,256]{2,1,0:T(8,128)(2,1)S(1)}, u32[]{:S(2)}, u32[]{:S(2)}) async-start(bf16[32,64,256]{2,1,0:T(8,128)(2,1)} %bitcast.9), calls=%async_computation.1 | async-start | bytes 2097152 | tf_op jit(solution)/shard_map/all_to_all | solution.py:399
  8.4 2.8 %shard_map.131 = bf16[8,2048]{1,0:T(8,128)(2,1)} custom-call(bf16[2048,256]{1,0:T(8,128)(2,1)} %head_ref.3, bf16[2048,256]{1,0:T(8,128)(2,1)} %flow_ref.3), custom_call_target="tpu_custom_call" | custom-call | tf_op jit(solution)/shard_map/pallas_call | solution.py:37
  11.3 0.8 fusion
  12.1 3.1 %collective-permute-start = (bf16[4,2048]{1,0:T(4,128)(2,1)S(1)}, bf16[4,2048]{1,0:T(4,128)(2,1)S(1)}, u32[]{:S(2)}, u32[]{:S(2)}) collective-permute-start(bf16[4,2048]{1,0:T(4,128)(2,1)S(1)} %get-tuple-element.10), channel_id=1, source_target_pairs={{8,0},{16,8},{24,16},{32,24},{40,32},{48,40},{56,48},{64,56},{72,6... | collective-permute-start | bytes 49160 | tf_op jit(solution)/shard_map/ppermute | solution.py:422
  15.2 4.2 %collective-permute-start.1 = (bf16[4,2048]{1,0:T(4,128)(2,1)S(1)}, bf16[4,2048]{1,0:T(4,128)(2,1)S(1)}, u32[]{:S(2)}, u32[]{:S(2)}) collective-permute-start(bf16[4,2048]{1,0:T(4,128)(2,1)S(1)} %get-tuple-element.11), channel_id=1, source_target_pairs={{0,8},{8,16},{16,24},{24,32},{32,40},{40,48},{48,56},{56,64},{64,7... | collective-permute-start | bytes 49160 | tf_op jit(solution)/shard_map/ppermute | solution.py:423
  19.5 0.9 add_multiply_fusion
  20.4 0.9 broadcast_divide_fusion
  21.2 1.2 copy.29
  22.4 0.7 convert_element_type.10
  23.1 0.7 convert_element_type.11
  23.8 0.3 copy.31
  24.1 1.3 copy.30
  25.4 1.4 copy.36
  26.8 1.4 copy.32
  28.2 0.0 copy-done.6
  28.2 1.4 copy.33
  29.5 0.0 copy-done.7
  29.5 1.3 copy.34
  30.9 0.0 copy-done.8
  30.9 1.4 copy.35
  32.3 1.1 broadcast_in_dim.29
  33.3 7.1 %concatenate.6.table_ref = f32[2048,128]{1,0:T(8,128)} concatenate(f32[2048,8]{1,0:T(8,128)S(1)} %copy.29, f32[2048,8]{1,0:T(8,128)} %copy.30, f32[2048,8]{1,0:T(8,128)S(1)} %copy.31, f32[2048,1]{1,0:T(8,128)} %copy.32, f32[2048,1]{1,0:T(8,128)} %copy.33, f32[2048,1]{1,0:T(8,128)} %copy.34, f32[2048,1]{1,0:T(8,128)} %copy.35, f32[2048,1]{1,0:T(8,128)} %copy.36, ...), dimensions={1} | concatenate | bytes 2097152 | tf_op jit(solution)/shard_map/concatenate | solution.py:395
  40.5 0.0 collective-permute-done
  40.5 0.0 collective-permute-done.1
  40.5 0.6 pad_maximum_fusion.halo_ref
  41.1 25.5 %shard_map.132 = bf16[2048,256]{1,0:T(8,128)(2,1)} custom-call(f32[2048,128]{1,0:T(8,128)} %concatenate.6.table_ref, bf16[2048,256]{1,0:T(8,128)(2,1)} %head_ref.3, bf16[2048,256]{1,0:T(8,128)(2,1)} %flow_ref.3, bf16[8,2048]{1,0:T(8,128)(2,1)} %pad_maximum_fusion.halo_ref), custom_call_target="tpu_custom_call" | custom-call | flops 31457280 | bytes 4194304 | tf_op jit(solution)/shard_map/pallas_call | solution.py:132
  66.6 0.0 all-to-all-done.1.rows_ref
  66.6 19.5 %all-to-all-start = ((bf16[32,64,256]{2,1,0:T(8,128)(2,1)}), bf16[32,64,256]{2,1,0:T(8,128)(2,1)S(1)}, u32[]{:S(2)}, u32[]{:S(2)}) async-start(bf16[32,64,256]{2,1,0:T(8,128)(2,1)} %bitcast.10), calls=%async_computation | async-start | bytes 2097152 | tf_op jit(solution)/shard_map/all_to_all | solution.py:399
  86.1 0.8 dynamic_slice.3
  86.8 0.1 broadcast_in_dim.30.begin_ref
  86.9 4.1 %shard_map.133 = (bf16[256,1024]{1,0:T(8,128)(2,1)S(1)}, bf16[256,1024]{1,0:T(8,128)(2,1)S(1)}, f32[256,1024]{1,0:T(8,128)S(1)}, f32[256,1024]{1,0:T(8,128)S(1)}) custom-call(bf16[32,64,256]{2,1,0:T(8,128)(2,1)S(1)} %all-to-all-done.1.rows_ref, s32[64,128]{1,0:T(8,128)S(1)} %broadcast_in_dim.30.begin_ref, bf16[2,1024,1024]{2,1,0:T(8,128)(2,1)} %weights_ref.3), custom_call_target="tpu_custom_call" | custom-call | flops 1073741824 | bytes 8388608 | tf_op jit(solution)/shard_map/pallas_call | solution.py:189
  91.1 0.0 copy-start
  91.1 1.0 copy-done
  92.0 0.0 copy-start.2
  92.0 0.8 copy-done.2
  92.9 0.0 copy-start.4
  92.9 0.8 copy-done.4
  93.7 7.8 %all-to-all-done.rows_ref = bf16[32,64,256]{2,1,0:T(8,128)(2,1)S(1)} async-done(((bf16[32,64,256]{2,1,0:T(8,128)(2,1)}), bf16[32,64,256]{2,1,0:T(8,128)(2,1)S(1)}, u32[]{:S(2)}, u32[]{:S(2)}) %all-to-all-start) | async-done | bytes 1048608 | tf_op jit(solution)/shard_map/all_to_all | solution.py:399
  101.5 0.0 copy-start.1
  101.5 1.2 copy-done.1
  102.7 0.0 copy-start.3
  102.7 1.0 copy-done.3
  103.7 0.0 copy-start.5
  103.8 1.0 copy-done.5
  104.8 8.1 %shard_map.134 = f32[2,1024,1024]{2,1,0:T(8,128)} custom-call(bf16[32,64,256]{2,1,0:T(8,128)(2,1)S(1)} %all-to-all-done.rows_ref, s32[64,128]{1,0:T(8,128)S(1)} %broadcast_in_dim.30.begin_ref, bf16[2,1024,1024]{2,1,0:T(8,128)(2,1)} %weights_ref.3, bf16[256,1024]{1,0:T(8,128)(2,1)S(1)} %copy-done.3, bf16[256,1024]{1,0:T(8,128)(2,1)S(1)} %copy-done.5, ...), custom_call_target="tpu_custom_call" | custom-call | flops 1610612736 | bytes 16777216 | tf_op jit(solution)/shard_map/pallas_call | solution.py:216
  112.8 60.2 %shard_map.135 = f32[2,4,1024]{2,1,0:T(4,128)} custom-call(f32[16,2,64,1024]{3,2,1,0:T(8,128)} %bitcast.8), custom_call_target="tpu_custom_call" | custom-call | tf_op jit(solution)/shard_map/pallas_call | solution.py:357
  173.1 1.4 copy.38
Async XLA Ops:
  0.6 27.5 %copy-start.6 = (f32[2048]{0:T(1024)S(1)}, f32[2048]{0:T(1024)}, u32[]{:S(2)}) copy-start(f32[2048]{0:T(1024)} %param.19) | copy-start | bytes 24580
  0.6 28.9 %copy-start.7 = (f32[2048]{0:T(1024)S(1)}, f32[2048]{0:T(1024)}, u32[]{:S(2)}) copy-start(f32[2048]{0:T(1024)} %param.20) | copy-start | bytes 24580
  0.7 30.2 %copy-start.8 = (f32[2048]{0:T(1024)S(1)}, f32[2048]{0:T(1024)}, u32[]{:S(2)}) copy-start(f32[2048]{0:T(1024)} %param.21) | copy-start | bytes 24580
  0.7 65.9 %all-to-all-start.1 = ((bf16[32,64,256]{2,1,0:T(8,128)(2,1)}), bf16[32,64,256]{2,1,0:T(8,128)(2,1)S(1)}, u32[]{:S(2)}, u32[]{:S(2)}) async-start(bf16[32,64,256]{2,1,0:T(8,128)(2,1)} %bitcast.9), calls=%async_computation.1 | async-start | bytes 2097152 | tf_op jit(solution)/shard_map/all_to_all | solution.py:399
  12.1 28.4 %collective-permute-start = (bf16[4,2048]{1,0:T(4,128)(2,1)S(1)}, bf16[4,2048]{1,0:T(4,128)(2,1)S(1)}, u32[]{:S(2)}, u32[]{:S(2)}) collective-permute-start(bf16[4,2048]{1,0:T(4,128)(2,1)S(1)} %get-tuple-element.10), channel_id=1, source_target_pairs={{8,0},{16,8},{24,16},{32,24},{40,32},{48,40},{56,48},{64,56},{72,6... | collective-permute-start | bytes 49160 | tf_op jit(solution)/shard_map/ppermute | solution.py:422
  15.2 25.2 %collective-permute-start.1 = (bf16[4,2048]{1,0:T(4,128)(2,1)S(1)}, bf16[4,2048]{1,0:T(4,128)(2,1)S(1)}, u32[]{:S(2)}, u32[]{:S(2)}) collective-permute-start(bf16[4,2048]{1,0:T(4,128)(2,1)S(1)} %get-tuple-element.11), channel_id=1, source_target_pairs={{0,8},{8,16},{16,24},{24,32},{32,40},{40,48},{48,56},{56,64},{64,7... | collective-permute-start | bytes 49160 | tf_op jit(solution)/shard_map/ppermute | solution.py:423
  66.6 34.9 %all-to-all-start = ((bf16[32,64,256]{2,1,0:T(8,128)(2,1)}), bf16[32,64,256]{2,1,0:T(8,128)(2,1)S(1)}, u32[]{:S(2)}, u32[]{:S(2)}) async-start(bf16[32,64,256]{2,1,0:T(8,128)(2,1)} %bitcast.10), calls=%async_computation | async-start | bytes 2097152 | tf_op jit(solution)/shard_map/all_to_all | solution.py:399
  91.1 1.0 copy-start
  92.0 0.8 copy-start.2
  92.9 0.8 copy-start.4
  101.5 1.2 copy-start.1
  102.7 1.0 copy-start.3
  103.7 1.0 copy-start.5

commit v2 on v0

v2 whole, which is shorter than its diff:
```python
import functools
import jax
import jax.numpy as jnp
from jax import lax
from jax.experimental import pallas as pl
from jax.experimental.pallas import tpu as pltpu
from jax.sharding import PartitionSpec as P

MESH = pl.DeviceIdType.MESH
PLANE = 32
CELLS = 8192
BF16 = jnp.bfloat16
F32 = jnp.float32
I16 = jnp.int16
TOP = 32767.0


def dot(lhs, rhs, lhs_dim, rhs_dim):
    return lax.dot_general(
        lhs, rhs, (((lhs_dim,), (rhs_dim,)), ((), ())), preferred_element_type=F32
    )


def iota(shape, dim):
    return lax.broadcasted_iota(jnp.int32, shape, dim)


def eye(size):
    return jnp.where(iota((size, size), 0) == iota((size, size), 1), 1.0, 0.0).astype(BF16)


W_LO, W_HI, L_LO, L_HI, H_LO, H_HI, FIRST, COUNT, END_A, END_L, END_Q, UPPER = range(12)


def prepare_params(position, imp_ref, fric_ref, junc_ref, count_ref, kind_ref, up_ref, down_ref, open_ref, prm):
    wide = imp_ref.shape
    imp = imp_ref[...]
    loss = fric_ref[...] * (1.0 + junc_ref[...].astype(F32))
    count = count_ref[...]
    before = position * 256 - 1
    section = lax.shift_right_logical(jnp.maximum(before, 0) * count, 13)
    row = iota(wide, 0)

    def pick(values, number):
        return jnp.sum(jnp.where(row == number, values, 0.0), axis=0, keepdims=True)

    w_lo, w_hi = pick(imp, section), pick(imp, section + 1)
    w_end = pick(imp, count - 1)
    prm[W_LO : W_LO + 1] = w_lo
    prm[W_HI : W_HI + 1] = w_hi
    prm[L_LO : L_LO + 1] = pick(loss, section)
    prm[L_HI : L_HI + 1] = pick(loss, section + 1)
    prm[H_LO : H_LO + 1] = 0.5 / w_lo
    prm[H_HI : H_HI + 1] = 0.5 / jnp.where(w_hi == 0.0, 1.0, w_hi)
    prm[FIRST : FIRST + 1] = (before * count - (section + 1) * CELLS).astype(F32)
    prm[COUNT : COUNT + 1] = count.astype(F32)
    kind, valve = kind_ref[...], open_ref[...]
    factor = 1.0 / (1.0 + w_end * valve)
    prm[END_A : END_A + 1] = jnp.where(kind == 0, 0.0, jnp.where(kind == 1, 1.0, factor))
    prm[END_L : END_L + 1] = jnp.where(kind == 0, down_ref[...], 0.0)
    prm[END_Q : END_Q + 1] = jnp.where(kind == 0, 1.0 / w_end, jnp.where(kind == 1, 0.0, valve * factor))
    prm[UPPER : UPPER + 1] = up_ref[...]


def stencil_tile(position, tile, prm, heads, flows, h1, q1, turned):
    lanes = pl.ds(pl.multiple_of(tile * 128, 128), 128)

    def param(number, rows=8):
        return jnp.broadcast_to(prm[number : number + 1, lanes], (rows, 128))

    count = param(COUNT)
    start = param(FIRST) + iota((8, 128), 0).astype(F32) * count
    lows = [param(W_LO), param(L_LO), param(H_LO)]
    highs = [param(W_HI), param(L_HI), param(H_HI)]

    def fields(value, number):
        high = value >= 0.0
        return [jnp.where(high, highs[k], lows[k]) for k in range(number)]

    def ends(lh, lq, rh, rq, wave, loss):
        forward = lh + lq * (wave - loss * jnp.abs(lq))
        backward = rh - rq * (wave - loss * jnp.abs(rq))
        return forward, backward

    def first(g, value):
        wave, loss, half = fields(value, 3)
        left, right = pl.ds(8 * g + 6, 8), pl.ds(8 * g + 8, 8)
        forward, backward = ends(
            heads[tile, left, :], flows[tile, left, :], heads[tile, right, :], flows[tile, right, :], wave, loss
        )
        return forward, backward, half

    value = start
    for g in range(33):
        forward, backward, half = first(g, value)
        h1[8 * g : 8 * g + 8] = 0.5 * (forward + backward)
        q1[8 * g : 8 * g + 8] = (forward - backward) * half
        value = value + 8.0 * count

    @pl.when(position == 0)
    def _():
        _, backward, half = first(0, start)
        upper = param(UPPER)
        at = iota((8, 128), 0) == 1
        h1[0:8] = jnp.where(at, upper, h1[0:8])
        q1[0:8] = jnp.where(at, (upper - backward) * (2.0 * half), q1[0:8])

    @pl.when(position == PLANE - 1)
    def _():
        forward, _, _ = first(32, start + 256.0 * count)
        at = iota((8, 128), 0) == 0
        h1[256:264] = jnp.where(at, param(END_A) * forward + param(END_L), h1[256:264])
        q1[256:264] = jnp.where(at, (forward - param(END_L)) * param(END_Q), q1[256:264])

    def second(g, value):
        wave, loss = fields(value, 2)
        left, right = pl.ds(8 * g, 8), pl.ds(8 * g + 2, 8)
        return ends(h1[left, :], q1[left, :], h1[right, :], q1[right, :], wave, loss)

    value = start + count
    for g in range(16):
        pieces = []
        for _ in range(2):
            forward, backward = second(2 * g + len(pieces), value)
            pieces.append(0.5 * (forward + backward))
            value = value + 8.0 * count
        turned[16 * g : 16 * g + 16] = jnp.concatenate(pieces, axis=0).astype(BF16)

    @pl.when(position == 0)
    def _():
        at = iota((16, 128), 0) == 0
        turned[0:16] = jnp.where(at, param(UPPER, 16), turned[0:16].astype(F32)).astype(BF16)

    @pl.when(position == PLANE - 1)
    def _():
        forward, _ = second(31, start + 249.0 * count)
        last = param(END_A) * forward + param(END_L)
        last = jnp.concatenate([last, last], axis=0)
        at = iota((16, 128), 0) == 15
        turned[240:256] = jnp.where(at, last, turned[240:256].astype(F32)).astype(BF16)


def cut_windows(rows_ref, begin_ref, out_ref):
    def group(number, carry):
        here = pl.ds(pl.multiple_of(number * 16, 16), 16)
        begin = begin_ref[here, :]
        block = lax.shift_right_logical(begin, 7)
        rest = begin & 127
        lane = iota((16, 128), 1)
        values = []
        for source in range(PLANE):
            pair = rows_ref[source, here, :].astype(F32)
            values += [pair[:, :128], pair[:, 128:]]
        for bit, count in ((32, 64), (16, 48), (8, 40), (4, 36), (2, 34), (1, 33)):
            on = (block & bit) != 0
            values = [
                jnp.where(on, values[j + bit], values[j]) if j + bit < len(values) else values[j]
                for j in range(count)
            ]
        index = (lane + rest) & 127
        keep = lane + rest < 128
        moved = [jnp.take_along_axis(v, index, axis=1) for v in values]
        for j in range(32):
            piece = jnp.where(keep, moved[j], moved[j + 1]).astype(BF16)
            at = pl.ds(pl.multiple_of((j // 8) * 64 + number * 16, 16), 16)
            out_ref[at, (j % 8) * 128 : (j % 8) * 128 + 128] = piece
        return carry

    lax.fori_loop(0, 4, group, 0)


def coded(block):
    top = jnp.maximum(jnp.max(jnp.abs(block), axis=0, keepdims=True), 1e-30)
    return jnp.round(block * (TOP / top)).astype(I16), top * (1.0 / TOP)


def decoded(number_ref, scale_ref, index):
    return number_ref[index].astype(F32) * scale_ref[index]


def kernel(
    scale,
    head_ref, flow_ref, imp_ref, fric_ref, junc_ref, count_ref, kind_ref, up_ref, down_ref, open_ref, begin_ref,
    weights_ref,
    end_ref, grads_ref,
    head, flow, weights, prm, halo_out, halo_in, heads, flows, h1, q1, turned, head_end,
    start_rows, end_rows, begin, a0, a1, z_val, out_val, targets, at_own, at_in, g_own, g_in,
    d_sum, sa, sas, ra, ras, sb, sbs, rb, rbs, a_sum, b_sum, sa2, sa2s, ra2, ra2s, sb2, sb2s, rb2, rb2s,
    z_sum, sz, szs, rz, rzs,
    lsem, hsend, hrecv, send1, recv1, send2, recv2, csend, crecv, rsend, rrecv,
):
    seg, samp, zpos = lax.axis_index("seg"), lax.axis_index("samp"), lax.axis_index("dp")
    y, xlo, core = seg // 4, (seg // 2) % 2, seg % 2
    x = samp * 2 + xlo
    position = seg * 2 + samp

    def at_plane(t):
        return {"seg": t // 2, "samp": t % 2}

    def at_x(t):
        return {"seg": y * 4 + (t % 2) * 2 + core, "samp": t // 2}

    def at_y(t):
        return {"seg": t * 4 + xlo * 2 + core}

    def at_z(t):
        return {"dp": t}

    at_core = {"seg": y * 4 + xlo * 2 + 1 - core}

    def remote(src, dst, send, recv, device):
        return pltpu.make_async_remote_copy(
            src_ref=src, dst_ref=dst, send_sem=send, recv_sem=recv, device_id=device, device_id_type=MESH
        )

    load_head = pltpu.make_async_copy(head_ref, head, lsem.at[0])
    load_flow = pltpu.make_async_copy(flow_ref, flow, lsem.at[1])
    load_weights = pltpu.make_async_copy(weights_ref, weights, lsem.at[2])
    load_head.start()
    load_flow.start()
    load_weights.start()

    barrier = pltpu.get_barrier_semaphore()

    def greet(p, c):
        pl.semaphore_signal(barrier, inc=1, device_id=at_plane((position + p) % PLANE), device_id_type=MESH)
        return c

    lax.fori_loop(1, PLANE, greet, 0)

    def greet_z(p, c):
        pl.semaphore_signal(barrier, inc=1, device_id=at_z((zpos + p) % 8), device_id_type=MESH)
        return c

    lax.fori_loop(1, 8, greet_z, 0)

    prepare_params(position, imp_ref, fric_ref, junc_ref, count_ref, kind_ref, up_ref, down_ref, open_ref, prm)
    lanes = pl.ds(pl.multiple_of((position // 2) * 128, 128), 128)
    own_begin = jnp.broadcast_to(begin_ref[:, lanes].astype(F32), (64, 128))
    chosen = iota((64, 128), 1) == iota((64, 128), 0) + (position % 2) * 64
    own_begin = jnp.sum(jnp.where(chosen, own_begin, 0.0), axis=1, keepdims=True)
    begin[...] = jnp.broadcast_to(own_begin, (64, 128)).astype(jnp.int32)

    halo_out[...] = jnp.zeros_like(halo_out)
    load_head.wait()
    load_flow.wait()
    unit = eye(256)

    def turn(t, c):
        rows = pl.ds(pl.multiple_of(t * 128, 128), 128)
        heads[t, 8:264, :] = dot(unit, head[rows, :], 1, 1)
        flows[t, 8:264, :] = dot(unit, flow[rows, :], 1, 1)
        lanes = pl.ds(pl.multiple_of(t * 128, 128), 128)
        halo_out[0, 0:2, lanes] = heads[t, 8:10, :]
        halo_out[0, 2:4, lanes] = flows[t, 8:10, :]
        halo_out[1, 0:2, lanes] = heads[t, 262:264, :]
        halo_out[1, 2:4, lanes] = flows[t, 262:264, :]
        return c

    lax.fori_loop(0, 16, turn, 0)

    pl.semaphore_wait(barrier, 38)

    below, above = (position + PLANE - 1) % PLANE, (position + 1) % PLANE
    halos = [
        remote(halo_out.at[0], halo_in.at[0], hsend.at[0], hrecv.at[0], at_plane(below)),
        remote(halo_out.at[1], halo_in.at[1], hsend.at[1], hrecv.at[1], at_plane(above)),
    ]
    for c in halos:
        c.start()

    def block(t):
        return pl.ds(pl.multiple_of(t * 64, 64), 64)

    def spread(source, target, send, recv, p):
        t = (position + p) % PLANE
        return remote(source.at[block(t)], target.at[position], send.at[p], recv.at[p], at_plane(t))

    def send_old(p, c):
        spread(head, start_rows, send1, recv1, p).start()
        return c

    lax.fori_loop(1, PLANE, send_old, 0)
    keep_old = pltpu.make_async_copy(head.at[block(position)], start_rows.at[position], lsem.at[3])
    keep_old.start()

    for c in halos:
        c.wait()

    small = eye(128)

    def one_tile(i, c):
        tile = (position // 2 + i) % 16
        lanes = pl.ds(pl.multiple_of(tile * 128, 128), 128)
        heads[tile, 264:266, :] = halo_in[0, 0:2, lanes]
        flows[tile, 264:266, :] = halo_in[0, 2:4, lanes]
        heads[tile, 6:8, :] = halo_in[1, 0:2, lanes]
        flows[tile, 6:8, :] = halo_in[1, 2:4, lanes]
        stencil_tile(position, tile, prm, heads, flows, h1, q1, turned)
        head_end[pl.ds(pl.multiple_of(tile * 128, 128), 128), :] = dot(small, turned[...], 1, 1).astype(BF16)
        for k in range(2):
            t = 2 * tile + k
            p = (t - position + PLANE) % PLANE

            @pl.when(p > 0)
            def _():
                spread(head_end, end_rows, send2, recv2, p).start()

        return c

    lax.fori_loop(0, 16, one_tile, 0)
    keep_new = pltpu.make_async_copy(head_end.at[block(position)], end_rows.at[position], lsem.at[4])
    keep_new.start()
    store_end = pltpu.make_async_copy(head_end, end_ref, lsem.at[5])
    store_end.start()

    load_weights.wait()
    keep_old.wait()

    def wait_old(p, c):
        spread(head, start_rows, send1, recv1, p).wait()
        return c

    lax.fori_loop(1, PLANE, wait_old, 0)
    cut_windows(start_rows, begin, a0)
    for c in range(4):
        cols = slice(c * 256, c * 256 + 256)
        z = dot(a0[...], weights[0, :, cols], 1, 0)
        z_val[:, cols] = z
        a1[:, cols] = (z * jax.nn.sigmoid(z)).astype(BF16)
    for c in range(4):
        cols = slice(c * 256, c * 256 + 256)
        out_val[:, cols] = dot(a1[...], weights[1, :, cols], 1, 0)

    def turn_a(b, c):
        cols = pl.ds(pl.multiple_of(b * 128, 128), 128)
        for layer, source in ((0, a0), (1, a1)):
            both = source[:, cols].T
            at_own[layer, b, 0] = both[0:64]
            at_own[layer, b, 1] = both[64:128]
        return c

    lax.fori_loop(0, 8, turn_a, 0)
    core_a = remote(at_own.at[:, :, 1 - core], at_in, csend.at[0], crecv.at[0], at_core)
    core_a.start()

    keep_new.wait()

    def wait_new(p, c):
        spread(head_end, end_rows, send2, recv2, p).wait()
        return c

    lax.fori_loop(1, PLANE, wait_new, 0)
    cut_windows(end_rows, begin, targets)
    g_own[1] = ((out_val[...] - targets[...].astype(F32)) * scale).astype(BF16)
    core_g1 = remote(g_own.at[1], g_in.at[1], csend.at[1], crecv.at[1], at_core)
    core_g1.start()
    for c in range(4):
        cols = slice(c * 256, c * 256 + 256)
        back = dot(g_own[1], weights[1, cols, :], 1, 1)
        z = z_val[:, cols]
        sigma = jax.nn.sigmoid(z)
        g_own[0, :, cols] = (back * sigma * (1.0 + z * (1.0 - sigma))).astype(BF16)
    core_g0 = remote(g_own.at[0], g_in.at[0], csend.at[2], crecv.at[2], at_core)
    core_g0.start()
    core_a.wait()
    core_g1.wait()

    copies = []
    for layer in (1, 0):
        if layer == 0:
            core_g0.wait()

        def one_block(b, c, layer=layer):
            d = dot(at_own[layer, b, core], g_own[layer], 1, 0) + dot(at_in[layer, b], g_in[layer], 1, 0)
            d_sum[layer * 8 + b] = d
            yy, xx = b // 2, b % 2
            for hi in range(2):
                numbers, scales = coded(d[hi * 32 : hi * 32 + 32, 0:512])
                sa[hi * 2 + xx, layer * 4 + yy] = numbers
                sas[hi * 2 + xx, layer * 4 + yy] = scales
                numbers, scales = coded(d[hi * 32 : hi * 32 + 32, 512:1024])
                sb[yy, layer * 4 + hi * 2 + xx] = numbers
                sbs[yy, layer * 4 + hi * 2 + xx] = scales
            return c

        lax.fori_loop(0, 8, one_block, 0)
        part = pl.ds(layer * 4, 4)
        for p in range(1, 4):
            tx, ty = (x + p) % 4, (y + p) % 4
            k = (layer * 3 + p - 1) * 4
            copies += [
                remote(sa.at[tx, part], ra.at[p - 1, part], rsend.at[k], rrecv.at[k], at_x(tx)),
                remote(sas.at[tx, part], ras.at[p - 1, part], rsend.at[k + 1], rrecv.at[k + 1], at_x(tx)),
                remote(sb.at[ty, part], rb.at[p - 1, part], rsend.at[k + 2], rrecv.at[k + 2], at_y(ty)),
                remote(sbs.at[ty, part], rbs.at[p - 1, part], rsend.at[k + 3], rrecv.at[k + 3], at_y(ty)),
            ]
        for c in copies[-12:]:
            c.start()
    for c in copies:
        c.wait()

    own_rows = pl.ds(pl.multiple_of(samp * 32, 32), 32)

    def add_first(i, c):
        layer, rest = i // 4, i % 4
        left = d_sum[layer * 8 + rest * 2 + xlo, own_rows, 0:512]
        high = pl.ds(pl.multiple_of((rest // 2) * 32, 32), 32)
        right = d_sum[layer * 8 + y * 2 + rest % 2, high, 512:1024]
        for p in range(3):
            left = left + ra[p, i].astype(F32) * ras[p, i]
            right = right + rb[p, i].astype(F32) * rbs[p, i]
        a_sum[i] = left
        b_sum[i] = right
        sa2[rest, layer], sa2s[rest, layer] = coded(left)
        sb2[rest, layer], sb2s[rest, layer] = coded(right)
        return c

    lax.fori_loop(0, 8, add_first, 0)
    copies = []
    for p in range(1, 4):
        tx, ty = (x + p) % 4, (y + p) % 4
        k = 24 + (p - 1) * 4
        copies += [
            remote(sa2.at[ty], ra2.at[p - 1], rsend.at[k], rrecv.at[k], at_y(ty)),
            remote(sa2s.at[ty], ra2s.at[p - 1], rsend.at[k + 1], rrecv.at[k + 1], at_y(ty)),
            remote(sb2.at[tx], rb2.at[p - 1], rsend.at[k + 2], rrecv.at[k + 2], at_x(tx)),
            remote(sb2s.at[tx], rb2s.at[p - 1], rsend.at[k + 3], rrecv.at[k + 3], at_x(tx)),
        ]
    for c in copies:
        c.start()
    for c in copies:
        c.wait()

    for layer in range(2):
        left = a_sum[layer * 4 + y]
        right = b_sum[layer * 4 + x]
        for p in range(3):
            left = left + ra2[p, layer].astype(F32) * ra2s[p, layer]
            right = right + rb2[p, layer].astype(F32) * rb2s[p, layer]
        for t in range(8):
            z_sum[t, 4 * layer : 4 * layer + 4] = left[4 * t : 4 * t + 4]
            z_sum[t, 8 + 4 * layer : 12 + 4 * layer] = right[4 * t : 4 * t + 4]
    for t in range(8):
        sz[t], szs[t] = coded(z_sum[t])
    copies = []
    for p in range(1, 8):
        t = (zpos + p) % 8
        k = 36 + (p - 1) * 2
        copies += [
            remote(sz.at[t], rz.at[p - 1], rsend.at[k], rrecv.at[k], at_z(t)),
            remote(szs.at[t], rzs.at[p - 1], rsend.at[k + 1], rrecv.at[k + 1], at_z(t)),
        ]
    for c in copies:
        c.start()
    for c in copies:
        c.wait()
    total = z_sum[zpos]
    for p in range(7):
        total = total + rz[p].astype(F32) * rzs[p]
    for layer in range(2):
        grads_ref[layer, :, 0:512] = total[4 * layer : 4 * layer + 4]
        grads_ref[layer, :, 512:1024] = total[8 + 4 * layer : 12 + 4 * layer]
    store_end.wait()


def whole(scale, *operands):
    hbm = pl.BlockSpec(memory_space=pl.ANY)
    vmem = pl.BlockSpec(memory_space=pltpu.VMEM)
    dma = pltpu.SemaphoreType.DMA
    return pl.pallas_call(
        functools.partial(kernel, scale),
        out_shape=[
            jax.ShapeDtypeStruct((2048, 256), BF16),
            jax.ShapeDtypeStruct((2, 4, 1024), F32),
        ],
        in_specs=[hbm, hbm] + [vmem] * 9 + [hbm],
        out_specs=[hbm, vmem],
        scratch_shapes=[
            pltpu.VMEM((2048, 256), BF16),
            pltpu.VMEM((2048, 256), BF16),
            pltpu.VMEM((2, 1024, 1024), BF16),
            pltpu.VMEM((16, 2048), F32),
            pltpu.VMEM((2, 8, 2048), F32),
            pltpu.VMEM((2, 8, 2048), F32),
            pltpu.VMEM((16, 272, 128), F32),
            pltpu.VMEM((16, 272, 128), F32),
            pltpu.VMEM((264, 128), F32),
            pltpu.VMEM((264, 128), F32),
            pltpu.VMEM((256, 128), BF16),
            pltpu.VMEM((2048, 256), BF16),
            pltpu.VMEM((32, 64, 256), BF16),
            pltpu.VMEM((32, 64, 256), BF16),
            pltpu.VMEM((64, 128), jnp.int32),
            pltpu.VMEM((256, 1024), BF16),
            pltpu.VMEM((256, 1024), BF16),
            pltpu.VMEM((256, 1024), F32),
            pltpu.VMEM((256, 1024), F32),
            pltpu.VMEM((256, 1024), BF16),
            pltpu.VMEM((2, 8, 2, 64, 256), BF16),
            pltpu.VMEM((2, 8, 64, 256), BF16),
            pltpu.VMEM((2, 256, 1024), BF16),
            pltpu.VMEM((2, 256, 1024), BF16),
            pltpu.VMEM((16, 64, 1024), F32),
            pltpu.VMEM((4, 8, 32, 512), I16),
            pltpu.VMEM((4, 8, 1, 512), F32),
            pltpu.VMEM((3, 8, 32, 512), I16),
            pltpu.VMEM((3, 8, 1, 512), F32),
            pltpu.VMEM((4, 8, 32, 512), I16),
            pltpu.VMEM((4, 8, 1, 512), F32),
            pltpu.VMEM((3, 8, 32, 512), I16),
            pltpu.VMEM((3, 8, 1, 512), F32),
            pltpu.VMEM((8, 32, 512), F32),
            pltpu.VMEM((8, 32, 512), F32),
            pltpu.VMEM((4, 2, 32, 512), I16),
            pltpu.VMEM((4, 2, 1, 512), F32),
            pltpu.VMEM((3, 2, 32, 512), I16),
            pltpu.VMEM((3, 2, 1, 512), F32),
            pltpu.VMEM((4, 2, 32, 512), I16),
            pltpu.VMEM((4, 2, 1, 512), F32),
            pltpu.VMEM((3, 2, 32, 512), I16),
            pltpu.VMEM((3, 2, 1, 512), F32),
            pltpu.VMEM((8, 16, 512), F32),
            pltpu.VMEM((8, 16, 512), I16),
            pltpu.VMEM((8, 1, 512), F32),
            pltpu.VMEM((7, 16, 512), I16),
            pltpu.VMEM((7, 1, 512), F32),
            dma((8,)),
            dma((2,)),
            dma((2,)),
            dma((PLANE,)),
            dma((PLANE,)),
            dma((PLANE,)),
            dma((PLANE,)),
            dma((3,)),
            dma((3,)),
            dma((50,)),
            dma((50,)),
        ],
        compiler_params=pltpu.CompilerParams(
            collective_id=1, has_side_effects=True, vmem_limit_bytes=58 << 20
        ),
    )(*operands)


def body(
    head_start,
    flow_start,
    impedance,
    friction,
    seg_count,
    junction_code,
    boundary_code,
    head_up,
    head_down,
    opening,
    window_start,
    layer_weights,
):
    row_total = window_start.shape[0] * lax.axis_size("dp") * 4
    return tuple(
        whole(
            8.0 / row_total,
            head_start,
            flow_start,
            impedance.T,
            friction.T,
            junction_code.T,
            seg_count[None, :],
            boundary_code[None, :],
            head_up[None, :],
            head_down[None, :],
            opening[None, :],
            window_start[None, :],
            layer_weights,
        )
    )


def solution(mesh):
    placed = (
        P("dp", ("seg", "samp")),
        P("dp", ("seg", "samp")),
        P("dp", None),
        P("dp", None),
        P("dp"),
        P("dp", None),
        P("dp"),
        P("dp"),
        P("dp"),
        P("dp"),
        P("dp"),
        P(),
    )
    return jax.shard_map(
        body,
        mesh=mesh,
        in_specs=placed,
        out_specs=(P("dp", ("seg", "samp")), P(None, ("seg", "samp", "dp"), None)),
        check_vma=False,
    )
```

time: 757 us -> 81.7 us (0.11)
  local copies, waits for them, and re-layouts: 363 us -> 3.64 us
  waiting for transfers between devices: 285 us -> 0 us
  Pallas kernels: 0 us -> 77.2 us
  other arithmetic: 46.3 us -> 0 us
  starting transfers between devices: 27.1 us -> 0 us
  between operations: 14.4 us -> 0.64 us
  matrix products: 12.1 us -> 0 us
    gather x512 -> x0, local copies, waits for them, and re-layouts: 341 us -> none
    unnamed x2 -> x0, waiting for transfers between devices: 282 us -> none
    pallas_call x0 -> x1, Pallas kernels: none -> 77.2 us  [whole(): pl.pallas_call(functools.partial(kernel, scale), out_shape=[jax.ShapeDtyp...]
    another operation x5 -> x0, other arithmetic: 25.5 us -> none  [the longest x3 19.7 us: body(): state = jnp.stack([heads, flows])]
    all_to_all x2 -> x0, starting transfers between devices: 15 us -> none  [the longest x1 9.03 us: body(): lax.all_to_all(head_start, ('seg', 'samp'), split_axis=0, concat_axis=1,...]
    dot_general x4 -> x0, matrix products: 12.1 us -> none  [the longest x2 6.11 us: body(): jnp.dot(activations[layer_number].T, grad_rows, preferred_element_type=jn...]
    ppermute x4 -> x0, starting transfers between devices: 12 us -> none  [the longest x2 8.01 us: padded_2(): lax.ppermute(lax.slice_in_dim(block, block.shape[dim] - width, None, axis...]
    concatenate x2 -> x0, other arithmetic: 10.2 us -> none  [padded_2(): block = jnp.concatenate([low, block, high], axis=dim)]
  transfers between devices with their start and end apart: 7 -> 0, of which waited for: 2 -> 0; matrix products, arithmetic and copies ran while one was open for 34% -> 0% of each run, Pallas kernels for 0% -> 0%
where the time goes in v2:
time: 81.7 us; the launch traced here: 81.5 us
  Pallas kernels  77.2 us (94%)
  local copies, waits for them, and re-layouts  3.64 us (4%)
    pallas_call x1, Pallas kernels, whole(): pl.pallas_call(functools.partial(kernel, scale), out_shape=[jax.ShapeDtyp...  77.2 us
    unnamed x2, local copies, waits for them, and re-layouts  3.64 us

profile of v2, /device:TPU:2, one launch (start us, length us, event | category | flops | bytes accessed | tf_op | source)
XLA Modules:
  0.0 81.5 jit_solution(1811510162876197739)
XLA Ops:
  0.6 77.2 %shard_map.131 = (bf16[2048,256]{1,0:T(8,128)(2,1)}, f32[2,4,1024]{2,1,0:T(4,128)}) custom-call(bf16[2048,256]{1,0:T(8,128)(2,1)} %head_ref.1, bf16[2048,256]{1,0:T(8,128)(2,1)} %flow_ref.1, f32[8,2048]{1,0:T(8,128)} %bitcast.9, f32[8,2048]{1,0:T(8,128)} %bitcast.10, s32[8,2048]{1,0:T(8,128)} %bitcast.11, s32[1,2048]{1,0:T(1,128)} %bitcast.12, ...), custom_call_target="tpu_custom_call" | custom-call | tf_op jit(solution)/shard_map/pallas_call | solution.py:471
  77.9 2.3 %copy.16 = bf16[2048,256]{1,0:T(8,128)(2,1)} copy(bf16[2048,256]{1,0:T(8,128)(2,1)} %get-tuple-element.4) | data formatting | bytes 2097152
  80.1 1.4 %copy.17 = f32[2,4,1024]{2,1,0:T(4,128)} copy(f32[2,4,1024]{2,1,0:T(4,128)} %get-tuple-element.5) | data formatting | bytes 65536

commit v3 on v2

--- a/solution.py
+++ b/solution.py
@@ -23,6 +23,16 @@
 
 def iota(shape, dim):
     return lax.broadcasted_iota(jnp.int32, shape, dim)
+
+
+def far_first():
+    offsets = [(dy, dx, dc) for dy in range(4) for dx in range(4) for dc in range(2)][1:]
+
+    def key(offset):
+        dy, dx, dc = offset
+        return (min(dy, 4 - dy) + min(dx, 4 - dx), dc, (dx * 7 + dy * 3) % 5)
+
+    return sorted(offsets, key=key, reverse=True)
 
 
 def eye(size):
@@ -234,30 +244,17 @@
 
     lax.fori_loop(1, 8, greet_z, 0)
 
-    prepare_params(position, imp_ref, fric_ref, junc_ref, count_ref, kind_ref, up_ref, down_ref, open_ref, prm)
-    lanes = pl.ds(pl.multiple_of((position // 2) * 128, 128), 128)
-    own_begin = jnp.broadcast_to(begin_ref[:, lanes].astype(F32), (64, 128))
-    chosen = iota((64, 128), 1) == iota((64, 128), 0) + (position % 2) * 64
-    own_begin = jnp.sum(jnp.where(chosen, own_begin, 0.0), axis=1, keepdims=True)
-    begin[...] = jnp.broadcast_to(own_begin, (64, 128)).astype(jnp.int32)
-
+    row, lane = iota((16, 256), 0), iota((16, 256), 1)
+    pick = jnp.where((row < 4) & (lane == jnp.where(row < 2, row, row + 252)), 1.0, 0.0).astype(BF16)
     halo_out[...] = jnp.zeros_like(halo_out)
     load_head.wait()
+    edge = dot(pick, head[...], 1, 1)
+    halo_out[0, 0:2] = edge[0:2]
+    halo_out[1, 0:2] = edge[2:4]
     load_flow.wait()
-    unit = eye(256)
-
-    def turn(t, c):
-        rows = pl.ds(pl.multiple_of(t * 128, 128), 128)
-        heads[t, 8:264, :] = dot(unit, head[rows, :], 1, 1)
-        flows[t, 8:264, :] = dot(unit, flow[rows, :], 1, 1)
-        lanes = pl.ds(pl.multiple_of(t * 128, 128), 128)
-        halo_out[0, 0:2, lanes] = heads[t, 8:10, :]
-        halo_out[0, 2:4, lanes] = flows[t, 8:10, :]
-        halo_out[1, 0:2, lanes] = heads[t, 262:264, :]
-        halo_out[1, 2:4, lanes] = flows[t, 262:264, :]
-        return c
-
-    lax.fori_loop(0, 16, turn, 0)
+    edge = dot(pick, flow[...], 1, 1)
+    halo_out[0, 2:4] = edge[0:2]
+    halo_out[1, 2:4] = edge[2:4]
 
     pl.semaphore_wait(barrier, 38)
 
@@ -276,21 +273,38 @@
         t = (position + p) % PLANE
         return remote(source.at[block(t)], target.at[position], send.at[p], recv.at[p], at_plane(t))
 
-    def send_old(p, c):
-        spread(head, start_rows, send1, recv1, p).start()
-        return c
-
-    lax.fori_loop(1, PLANE, send_old, 0)
+    for dy, dx, dc in far_first():
+        tx = (x + dx) % 4
+        t = ((y + dy) % 4) * 8 + (tx % 2) * 4 + ((core + dc) % 2) * 2 + tx // 2
+        spread(head, start_rows, send1, recv1, (t - position + PLANE) % PLANE).start()
     keep_old = pltpu.make_async_copy(head.at[block(position)], start_rows.at[position], lsem.at[3])
     keep_old.start()
 
+    prepare_params(position, imp_ref, fric_ref, junc_ref, count_ref, kind_ref, up_ref, down_ref, open_ref, prm)
+    lanes = pl.ds(pl.multiple_of((position // 2) * 128, 128), 128)
+    own_begin = jnp.broadcast_to(begin_ref[:, lanes].astype(F32), (64, 128))
+    chosen = iota((64, 128), 1) == iota((64, 128), 0) + (position % 2) * 64
+    own_begin = jnp.sum(jnp.where(chosen, own_begin, 0.0), axis=1, keepdims=True)
+    begin[...] = jnp.broadcast_to(own_begin, (64, 128)).astype(jnp.int32)
+    unit = eye(256)
+
+    def turn(t, c):
+        rows = pl.ds(pl.multiple_of(t * 128, 128), 128)
+        heads[t, 8:264, :] = dot(unit, head[rows, :], 1, 1)
+        flows[t, 8:264, :] = dot(unit, flow[rows, :], 1, 1)
+        return c
+
+    lax.fori_loop(0, 16, turn, 0)
     for c in halos:
         c.wait()
 
     small = eye(128)
 
     def one_tile(i, c):
-        tile = (position // 2 + i) % 16
+        turn_y = i // 4
+        turn_y = jnp.where(turn_y < 2, 2 - turn_y, 6 - turn_y)
+        turn_y = jnp.where(i >= 12, 0, jnp.where(i >= 8, 3, turn_y))
+        tile = ((y + turn_y) % 4) * 4 + (xlo * 2 + core + i) % 4
         lanes = pl.ds(pl.multiple_of(tile * 128, 128), 128)
         heads[tile, 264:266, :] = halo_in[0, 0:2, lanes]
         flows[tile, 264:266, :] = halo_in[0, 2:4, lanes]
@@ -336,12 +350,12 @@
         cols = pl.ds(pl.multiple_of(b * 128, 128), 128)
         for layer, source in ((0, a0), (1, a1)):
             both = source[:, cols].T
-            at_own[layer, b, 0] = both[0:64]
-            at_own[layer, b, 1] = both[64:128]
+            at_own[layer, 0, b] = both[0:64]
+            at_own[layer, 1, b] = both[64:128]
         return c
 
     lax.fori_loop(0, 8, turn_a, 0)
-    core_a = remote(at_own.at[:, :, 1 - core], at_in, csend.at[0], crecv.at[0], at_core)
+    core_a = remote(at_own.at[:, 1 - core], at_in, csend.at[0], crecv.at[0], at_core)
     core_a.start()
 
     keep_new.wait()
@@ -366,70 +380,99 @@
     core_a.wait()
     core_g1.wait()
 
-    copies = []
+    firsts = {}
     for layer in (1, 0):
         if layer == 0:
             core_g0.wait()
-
-        def one_block(b, c, layer=layer):
-            d = dot(at_own[layer, b, core], g_own[layer], 1, 0) + dot(at_in[layer, b], g_in[layer], 1, 0)
-            d_sum[layer * 8 + b] = d
-            yy, xx = b // 2, b % 2
-            for hi in range(2):
-                numbers, scales = coded(d[hi * 32 : hi * 32 + 32, 0:512])
-                sa[hi * 2 + xx, layer * 4 + yy] = numbers
-                sas[hi * 2 + xx, layer * 4 + yy] = scales
-                numbers, scales = coded(d[hi * 32 : hi * 32 + 32, 512:1024])
-                sb[yy, layer * 4 + hi * 2 + xx] = numbers
-                sbs[yy, layer * 4 + hi * 2 + xx] = scales
-            return c
-
-        lax.fori_loop(0, 8, one_block, 0)
         part = pl.ds(layer * 4, 4)
-        for p in range(1, 4):
-            tx, ty = (x + p) % 4, (y + p) % 4
-            k = (layer * 3 + p - 1) * 4
-            copies += [
-                remote(sa.at[tx, part], ra.at[p - 1, part], rsend.at[k], rrecv.at[k], at_x(tx)),
-                remote(sas.at[tx, part], ras.at[p - 1, part], rsend.at[k + 1], rrecv.at[k + 1], at_x(tx)),
-                remote(sb.at[ty, part], rb.at[p - 1, part], rsend.at[k + 2], rrecv.at[k + 2], at_y(ty)),
-                remote(sbs.at[ty, part], rbs.at[p - 1, part], rsend.at[k + 3], rrecv.at[k + 3], at_y(ty)),
-            ]
-        for c in copies[-12:]:
-            c.start()
-    for c in copies:
-        c.wait()
+        blocks = pl.ds(layer * 8, 8)
+        for side in range(2):
+            for c in (2 * side, 2 * side + 1):
+                cols = slice(c * 256, c * 256 + 256)
+                d = dot(at_own[layer, core].reshape(512, 256), g_own[layer, :, cols], 1, 0)
+                d = d + dot(at_in[layer].reshape(512, 256), g_in[layer, :, cols], 1, 0)
+                d_sum[blocks, :, cols] = d.reshape(8, 64, 256)
+
+            def code_left(b, c, layer=layer):
+                yy, xx = b // 2, b % 2
+                for hi in range(2):
+                    numbers, scales = coded(d_sum[layer * 8 + b, hi * 32 : hi * 32 + 32, 0:512])
+                    sa[hi * 2 + xx, layer * 4 + yy] = numbers
+                    sas[hi * 2 + xx, layer * 4 + yy] = scales
+                return c
+
+            def code_right(b, c, layer=layer):
+                yy, xx = b // 2, b % 2
+                for hi in range(2):
+                    numbers, scales = coded(d_sum[layer * 8 + b, hi * 32 : hi * 32 + 32, 512:1024])
+                    sb[yy, layer * 4 + hi * 2 + xx] = numbers
+                    sbs[yy, layer * 4 + hi * 2 + xx] = scales
+                return c
+
+            lax.fori_loop(0, 8, code_right if side else code_left, 0)
+            copies = []
+            for p in (2, 1, 3):
+                tx, ty = (x + p) % 4, (y + p) % 4
+                k = ((layer * 2 + side) * 3 + p - 1) * 2
+                if side == 0:
+                    copies += [
+                        remote(sa.at[tx, part], ra.at[p - 1, part], rsend.at[k], rrecv.at[k], at_x(tx)),
+                        remote(sas.at[tx, part], ras.at[p - 1, part], rsend.at[k + 1], rrecv.at[k + 1], at_x(tx)),
+                    ]
+                else:
+                    copies += [
+                        remote(sb.at[ty, part], rb.at[p - 1, part], rsend.at[k], rrecv.at[k], at_y(ty)),
+                        remote(sbs.at[ty, part], rbs.at[p - 1, part], rsend.at[k + 1], rrecv.at[k + 1], at_y(ty)),
+                    ]
+            for c in copies:
+                c.start()
+            firsts[layer, side] = copies
 
     own_rows = pl.ds(pl.multiple_of(samp * 32, 32), 32)
-
-    def add_first(i, c):
-        layer, rest = i // 4, i % 4
-        left = d_sum[layer * 8 + rest * 2 + xlo, own_rows, 0:512]
-        high = pl.ds(pl.multiple_of((rest // 2) * 32, 32), 32)
-        right = d_sum[layer * 8 + y * 2 + rest % 2, high, 512:1024]
-        for p in range(3):
-            left = left + ra[p, i].astype(F32) * ras[p, i]
-            right = right + rb[p, i].astype(F32) * rbs[p, i]
-        a_sum[i] = left
-        b_sum[i] = right
-        sa2[rest, layer], sa2s[rest, layer] = coded(left)
-        sb2[rest, layer], sb2s[rest, layer] = coded(right)
-        return c
-
-    lax.fori_loop(0, 8, add_first, 0)
-    copies = []
-    for p in range(1, 4):
-        tx, ty = (x + p) % 4, (y + p) % 4
-        k = 24 + (p - 1) * 4
-        copies += [
-            remote(sa2.at[ty], ra2.at[p - 1], rsend.at[k], rrecv.at[k], at_y(ty)),
-            remote(sa2s.at[ty], ra2s.at[p - 1], rsend.at[k + 1], rrecv.at[k + 1], at_y(ty)),
-            remote(sb2.at[tx], rb2.at[p - 1], rsend.at[k + 2], rrecv.at[k + 2], at_x(tx)),
-            remote(sb2s.at[tx], rb2s.at[p - 1], rsend.at[k + 3], rrecv.at[k + 3], at_x(tx)),
-        ]
-    for c in copies:
-        c.start()
-    for c in copies:
+    seconds = []
+    for layer in (1, 0):
+        for side in range(2):
+            for c in firsts[layer, side]:
+                c.wait()
+
+            def add_left(rest, c, layer=layer):
+                i = layer * 4 + rest
+                left = d_sum[layer * 8 + rest * 2 + xlo, own_rows, 0:512]
+                for p in range(3):
+                    left = left + ra[p, i].astype(F32) * ras[p, i]
+                a_sum[i] = left
+                sa2[rest, layer], sa2s[rest, layer] = coded(left)
+                return c
+
+            def add_right(rest, c, layer=layer):
+                i = layer * 4 + rest
+                high = pl.ds(pl.multiple_of((rest // 2) * 32, 32), 32)
+                right = d_sum[layer * 8 + y * 2 + rest % 2, high, 512:1024]
+                for p in range(3):
+                    right = right + rb[p, i].astype(F32) * rbs[p, i]
+                b_sum[i] = right
+                sb2[rest, layer], sb2s[rest, layer] = coded(right)
+                return c
+
+            lax.fori_loop(0, 4, add_right if side else add_left, 0)
+            copies = []
+            for p in (2, 1, 3):
+                tx, ty = (x + p) % 4, (y + p) % 4
+                k = 24 + ((layer * 2 + side) * 3 + p - 1) * 2
+                if side == 0:
+                    copies += [
+                        remote(sa2.at[ty, layer], ra2.at[p - 1, layer], rsend.at[k], rrecv.at[k], at_y(ty)),
+                        remote(sa2s.at[ty, layer], ra2s.at[p - 1, layer], rsend.at[k + 1], rrecv.at[k + 1], at_y(ty)),
+                    ]
+                else:
+                    copies += [
+                        remote(sb2.at[tx, layer], rb2.at[p - 1, layer], rsend.at[k], rrecv.at[k], at_x(tx)),
+                        remote(sb2s.at[tx, layer], rb2s.at[p - 1, layer], rsend.at[k + 1], rrecv.at[k + 1], at_x(tx)),
+                    ]
+            for c in copies:
+                c.start()
+            seconds += copies
+    for c in seconds:
         c.wait()
 
     for layer in range(2):
@@ -444,9 +487,9 @@
     for t in range(8):
         sz[t], szs[t] = coded(z_sum[t])
     copies = []
-    for p in range(1, 8):
+    for p in (4, 3, 5, 2, 6, 1, 7):
         t = (zpos + p) % 8
-        k = 36 + (p - 1) * 2
+        k = 48 + (p - 1) * 2
         copies += [
             remote(sz.at[t], rz.at[p - 1], rsend.at[k], rrecv.at[k], at_z(t)),
             remote(szs.at[t], rzs.at[p - 1], rsend.at[k + 1], rrecv.at[k + 1], at_z(t)),
@@ -497,7 +540,7 @@
             pltpu.VMEM((256, 1024), F32),
             pltpu.VMEM((256, 1024), F32),
             pltpu.VMEM((256, 1024), BF16),
-            pltpu.VMEM((2, 8, 2, 64, 256), BF16),
+            pltpu.VMEM((2, 2, 8, 64, 256), BF16),
             pltpu.VMEM((2, 8, 64, 256), BF16),
             pltpu.VMEM((2, 256, 1024), BF16),
             pltpu.VMEM((2, 256, 1024), BF16),
@@ -534,13 +577,45 @@
             dma((PLANE,)),
             dma((3,)),
             dma((3,)),
-            dma((50,)),
-            dma((50,)),
+            dma((62,)),
+            dma((62,)),
         ],
         compiler_params=pltpu.CompilerParams(
             collective_id=1, has_side_effects=True, vmem_limit_bytes=58 << 20
         ),
     )(*operands)
+
+
+def finish_kernel(end_ref, grads_ref, end_out, grads_out, held, totals, load_sem, store_sem):
+    parts = [pl.ds(i * 512, 512) for i in range(4)]
+    loads = [pltpu.make_async_copy(end_ref.at[r], held.at[r], load_sem.at[i]) for i, r in enumerate(parts)]
+    stores = [pltpu.make_async_copy(held.at[r], end_out.at[r], store_sem.at[i]) for i, r in enumerate(parts)]
+    loads.append(pltpu.make_async_copy(grads_ref, totals, load_sem.at[4]))
+    stores.append(pltpu.make_async_copy(totals, grads_out, store_sem.at[4]))
+    for c in loads:
+        c.start()
+    for load, store in zip(loads, stores):
+        load.wait()
+        store.start()
+    for c in stores:
+        c.wait()
+
+
+def finish(end, grads):
+    hbm = pl.BlockSpec(memory_space=pl.ANY)
+    return pl.pallas_call(
+        finish_kernel,
+        out_shape=[jax.ShapeDtypeStruct(end.shape, end.dtype), jax.ShapeDtypeStruct(grads.shape, grads.dtype)],
+        in_specs=[hbm, hbm],
+        out_specs=[hbm, hbm],
+        scratch_shapes=[
+            pltpu.VMEM(end.shape, end.dtype),
+            pltpu.VMEM(grads.shape, grads.dtype),
+            pltpu.SemaphoreType.DMA((5,)),
+            pltpu.SemaphoreType.DMA((5,)),
+        ],
+        compiler_params=pltpu.CompilerParams(vmem_limit_bytes=58 << 20),
+    )(end, grads)
 
 
 def body(
@@ -559,7 +634,8 @@
 ):
     row_total = window_start.shape[0] * lax.axis_size("dp") * 4
     return tuple(
-        whole(
+        finish(
+            *whole(
             8.0 / row_total,
             head_start,
             flow_start,
@@ -573,7 +649,7 @@
             opening[None, :],
             window_start[None, :],
             layer_weights,
-        )
+        ))
     )
 
 

time: 81.7 us -> 73.7 us (0.902)
  Pallas kernels: 77.2 us -> 72.6 us
  local copies, waits for them, and re-layouts: 3.64 us -> 0 us
    pallas_call x1, Pallas kernels: 77.2 us -> 70.6 us  [whole(): pl.pallas_call(functools.partial(kernel, scale), out_shape=[jax.ShapeDtyp...]
    unnamed x2 -> x0, local copies, waits for them, and re-layouts: 3.64 us -> none
    pallas_call x0 -> x1, Pallas kernels: none -> 2 us  [finish(): pl.pallas_call(finish_kernel, out_shape=[jax.ShapeDtypeStruct(end.shape,...]
where the time goes in v3:
time: 73.7 us; the launch traced here: 73.2 us
  Pallas kernels  72.6 us (99%)
    pallas_call x1, Pallas kernels, whole(): pl.pallas_call(functools.partial(kernel, scale), out_shape=[jax.ShapeDtyp...  70.6 us
    pallas_call x1, Pallas kernels, finish(): pl.pallas_call(finish_kernel, out_shape=[jax.ShapeDtypeStruct(end.shape,...  2 us

profile of v3, /device:TPU:2, one launch (start us, length us, event | category | flops | bytes accessed | tf_op | source)
XLA Modules:
  0.0 73.2 jit_solution(15100948717888310580)
XLA Ops:
  0.6 70.6 %shard_map.131 = (bf16[2048,256]{1,0:T(8,128)(2,1)}, f32[2,4,1024]{2,1,0:T(4,128)}) custom-call(bf16[2048,256]{1,0:T(8,128)(2,1)} %head_ref.1, bf16[2048,256]{1,0:T(8,128)(2,1)} %flow_ref.1, f32[8,2048]{1,0:T(8,128)} %bitcast.9, f32[8,2048]{1,0:T(8,128)} %bitcast.10, s32[8,2048]{1,0:T(8,128)} %bitcast.11, s32[1,2048]{1,0:T(1,128)} %bitcast.12, ...), custom_call_target="tpu_custom_call" | custom-call | tf_op jit(solution)/shard_map/pallas_call | solution.py:514
  71.2 2.0 %shard_map.132 = (bf16[2048,256]{1,0:T(8,128)(2,1)}, f32[2,4,1024]{2,1,0:T(4,128)}) custom-call(bf16[2048,256]{1,0:T(8,128)(2,1)} %get-tuple-element.4.end_ref, f32[2,4,1024]{2,1,0:T(4,128)} %get-tuple-element.5.grads_ref), custom_call_target="tpu_custom_call" | custom-call | tf_op jit(solution)/shard_map/pallas_call | solution.py:606

commit v4 on v3

--- a/solution.py
+++ b/solution.py
@@ -13,6 +13,7 @@
 F32 = jnp.float32
 I16 = jnp.int16
 TOP = 32767.0
+EARLY = 10
 
 
 def dot(lhs, rhs, lhs_dim, rhs_dim):
@@ -154,22 +155,22 @@
     def group(number, carry):
         here = pl.ds(pl.multiple_of(number * 16, 16), 16)
         begin = begin_ref[here, :]
-        block = lax.shift_right_logical(begin, 7)
+        block = lax.shift_right_logical(begin, 7).astype(I16)
         rest = begin & 127
         lane = iota((16, 128), 1)
         values = []
         for source in range(PLANE):
-            pair = rows_ref[source, here, :].astype(F32)
+            pair = rows_ref[source, here, :]
             values += [pair[:, :128], pair[:, 128:]]
         for bit, count in ((32, 64), (16, 48), (8, 40), (4, 36), (2, 34), (1, 33)):
-            on = (block & bit) != 0
+            on = (block & jnp.int16(bit)) != 0
             values = [
                 jnp.where(on, values[j + bit], values[j]) if j + bit < len(values) else values[j]
                 for j in range(count)
             ]
         index = (lane + rest) & 127
         keep = lane + rest < 128
-        moved = [jnp.take_along_axis(v, index, axis=1) for v in values]
+        moved = [jnp.take_along_axis(v.astype(F32), index, axis=1) for v in values]
         for j in range(32):
             piece = jnp.where(keep, moved[j], moved[j + 1]).astype(BF16)
             at = pl.ds(pl.multiple_of((j // 8) * 64 + number * 16, 16), 16)
@@ -190,14 +191,15 @@
 
 def kernel(
     scale,
-    head_ref, flow_ref, imp_ref, fric_ref, junc_ref, count_ref, kind_ref, up_ref, down_ref, open_ref, begin_ref,
-    weights_ref,
+    head_hbm, flow_hbm, imp_hbm, fric_hbm, junc_hbm, count_hbm, kind_hbm, up_hbm, down_hbm, open_hbm, begin_hbm,
+    weights_hbm,
     end_ref, grads_ref,
+    imp_ref, fric_ref, junc_ref, count_ref, kind_ref, up_ref, down_ref, open_ref, begin_ref,
     head, flow, weights, prm, halo_out, halo_in, heads, flows, h1, q1, turned, head_end,
     start_rows, end_rows, begin, a0, a1, z_val, out_val, targets, at_own, at_in, g_own, g_in,
-    d_sum, sa, sas, ra, ras, sb, sbs, rb, rbs, a_sum, b_sum, sa2, sa2s, ra2, ra2s, sb2, sb2s, rb2, rb2s,
+    d_sum, sf, sfs, rf, rfs, sn, sns, rn, rns, a_sum, b_sum, sa2, sa2s, ra2, ra2s, sb2, sb2s, rb2, rb2s,
     z_sum, sz, szs, rz, rzs,
-    lsem, hsend, hrecv, send1, recv1, send2, recv2, csend, crecv, rsend, rrecv,
+    lsem, halo_sem, old_sem, new_sem, csend, crecv, relay_sem, first_sem, early_send, second_sem, third_sem,
 ):
     seg, samp, zpos = lax.axis_index("seg"), lax.axis_index("samp"), lax.axis_index("dp")
     y, xlo, core = seg // 4, (seg // 2) % 2, seg % 2
@@ -207,6 +209,10 @@
     def at_plane(t):
         return {"seg": t // 2, "samp": t % 2}
 
+    def neighbour(offset):
+        tx = (x + offset[1]) % 4
+        return ((y + offset[0]) % 4) * 8 + (tx % 2) * 4 + ((core + offset[2]) % 2) * 2 + tx // 2
+
     def at_x(t):
         return {"seg": y * 4 + (t % 2) * 2 + core, "samp": t // 2}
 
@@ -223,63 +229,71 @@
             src_ref=src, dst_ref=dst, send_sem=send, recv_sem=recv, device_id=device, device_id_type=MESH
         )
 
-    load_head = pltpu.make_async_copy(head_ref, head, lsem.at[0])
-    load_flow = pltpu.make_async_copy(flow_ref, flow, lsem.at[1])
-    load_weights = pltpu.make_async_copy(weights_ref, weights, lsem.at[2])
-    load_head.start()
-    load_flow.start()
-    load_weights.start()
+    def take(ref, sem):
+        pltpu.make_async_copy(ref, ref, sem).wait()
 
     barrier = pltpu.get_barrier_semaphore()
 
-    def greet(p, c):
-        pl.semaphore_signal(barrier, inc=1, device_id=at_plane((position + p) % PLANE), device_id_type=MESH)
-        return c
-
-    lax.fori_loop(1, PLANE, greet, 0)
-
-    def greet_z(p, c):
+    for p in (4, 3, 5, 2, 6, 1, 7):
         pl.semaphore_signal(barrier, inc=1, device_id=at_z((zpos + p) % 8), device_id_type=MESH)
-        return c
-
-    lax.fori_loop(1, 8, greet_z, 0)
+    for offset in far_first():
+        pl.semaphore_signal(barrier, inc=1, device_id=at_plane(neighbour(offset)), device_id_type=MESH)
+
+    loads = [
+        pltpu.make_async_copy(source, target, lsem.at[3 + number])
+        for number, (source, target) in enumerate(
+            (
+                (head_hbm, head), (flow_hbm, flow), (imp_hbm, imp_ref), (fric_hbm, fric_ref), (junc_hbm, junc_ref),
+                (count_hbm, count_ref), (kind_hbm, kind_ref), (up_hbm, up_ref), (down_hbm, down_ref),
+                (open_hbm, open_ref), (begin_hbm, begin_ref), (weights_hbm, weights),
+            )
+        )
+    ]
+    for c in loads[:11]:
+        c.start()
+
+    pl.semaphore_wait(barrier, 38)
+
+    def block(t):
+        return pl.ds(pl.multiple_of(t * 64, 64), 64)
+
+    def spread(source, target, sem, t):
+        return remote(source.at[block(t)], target.at[position], sem.at[0], sem.at[1], at_plane(t))
+
+    def send_old(offset):
+        spread(head_hbm, start_rows, old_sem, neighbour(offset)).start()
+
+    for offset in far_first()[:EARLY]:
+        send_old(offset)
 
     row, lane = iota((16, 256), 0), iota((16, 256), 1)
     pick = jnp.where((row < 4) & (lane == jnp.where(row < 2, row, row + 252)), 1.0, 0.0).astype(BF16)
     halo_out[...] = jnp.zeros_like(halo_out)
-    load_head.wait()
+    loads[0].wait()
     edge = dot(pick, head[...], 1, 1)
     halo_out[0, 0:2] = edge[0:2]
     halo_out[1, 0:2] = edge[2:4]
-    load_flow.wait()
+    loads[1].wait()
     edge = dot(pick, flow[...], 1, 1)
     halo_out[0, 2:4] = edge[0:2]
     halo_out[1, 2:4] = edge[2:4]
 
-    pl.semaphore_wait(barrier, 38)
-
     below, above = (position + PLANE - 1) % PLANE, (position + 1) % PLANE
     halos = [
-        remote(halo_out.at[0], halo_in.at[0], hsend.at[0], hrecv.at[0], at_plane(below)),
-        remote(halo_out.at[1], halo_in.at[1], hsend.at[1], hrecv.at[1], at_plane(above)),
+        remote(halo_out.at[0], halo_in.at[0], halo_sem.at[0], halo_sem.at[1], at_plane(below)),
+        remote(halo_out.at[1], halo_in.at[1], halo_sem.at[0], halo_sem.at[1], at_plane(above)),
     ]
     for c in halos:
         c.start()
 
-    def block(t):
-        return pl.ds(pl.multiple_of(t * 64, 64), 64)
-
-    def spread(source, target, send, recv, p):
-        t = (position + p) % PLANE
-        return remote(source.at[block(t)], target.at[position], send.at[p], recv.at[p], at_plane(t))
-
-    for dy, dx, dc in far_first():
-        tx = (x + dx) % 4
-        t = ((y + dy) % 4) * 8 + (tx % 2) * 4 + ((core + dc) % 2) * 2 + tx // 2
-        spread(head, start_rows, send1, recv1, (t - position + PLANE) % PLANE).start()
-    keep_old = pltpu.make_async_copy(head.at[block(position)], start_rows.at[position], lsem.at[3])
+    for offset in far_first()[EARLY:]:
+        send_old(offset)
+    loads[11].start()
+    keep_old = pltpu.make_async_copy(head.at[block(position)], start_rows.at[position], lsem.at[0])
     keep_old.start()
 
+    for c in loads[2:11]:
+        c.wait()
     prepare_params(position, imp_ref, fric_ref, junc_ref, count_ref, kind_ref, up_ref, down_ref, open_ref, prm)
     lanes = pl.ds(pl.multiple_of((position // 2) * 128, 128), 128)
     own_begin = jnp.broadcast_to(begin_ref[:, lanes].astype(F32), (64, 128))
@@ -295,8 +309,7 @@
         return c
 
     lax.fori_loop(0, 16, turn, 0)
-    for c in halos:
-        c.wait()
+    take(halo_in, halo_sem.at[1])
 
     small = eye(128)
 
@@ -314,28 +327,23 @@
         head_end[pl.ds(pl.multiple_of(tile * 128, 128), 128), :] = dot(small, turned[...], 1, 1).astype(BF16)
         for k in range(2):
             t = 2 * tile + k
-            p = (t - position + PLANE) % PLANE
-
-            @pl.when(p > 0)
+
+            @pl.when(t != position)
             def _():
-                spread(head_end, end_rows, send2, recv2, p).start()
+                spread(head_end, end_rows, new_sem, t).start()
 
         return c
 
     lax.fori_loop(0, 16, one_tile, 0)
-    keep_new = pltpu.make_async_copy(head_end.at[block(position)], end_rows.at[position], lsem.at[4])
+    keep_new = pltpu.make_async_copy(head_end.at[block(position)], end_rows.at[position], lsem.at[1])
     keep_new.start()
-    store_end = pltpu.make_async_copy(head_end, end_ref, lsem.at[5])
+    store_end = pltpu.make_async_copy(head_end, end_ref, lsem.at[2])
     store_end.start()
 
-    load_weights.wait()
+    loads[11].wait()
     keep_old.wait()
 
-    def wait_old(p, c):
-        spread(head, start_rows, send1, recv1, p).wait()
-        return c
-
-    lax.fori_loop(1, PLANE, wait_old, 0)
+    take(start_rows.at[pl.ds(0, PLANE - 1)], old_sem.at[1])
     cut_windows(start_rows, begin, a0)
     for c in range(4):
         cols = slice(c * 256, c * 256 + 256)
@@ -360,11 +368,7 @@
 
     keep_new.wait()
 
-    def wait_new(p, c):
-        spread(head_end, end_rows, send2, recv2, p).wait()
-        return c
-
-    lax.fori_loop(1, PLANE, wait_new, 0)
+    take(end_rows.at[pl.ds(0, PLANE - 1)], new_sem.at[1])
     cut_windows(end_rows, begin, targets)
     g_own[1] = ((out_val[...] - targets[...].astype(F32)) * scale).astype(BF16)
     core_g1 = remote(g_own.at[1], g_in.at[1], csend.at[1], crecv.at[1], at_core)
@@ -377,103 +381,134 @@
         g_own[0, :, cols] = (back * sigma * (1.0 + z * (1.0 - sigma))).astype(BF16)
     core_g0 = remote(g_own.at[0], g_in.at[0], csend.at[2], crecv.at[2], at_core)
     core_g0.start()
-    core_a.wait()
-    core_g1.wait()
-
-    firsts = {}
+
+    def share(layer, side, target, i):
+        if side == 0:
+            return d_sum[layer * 8 + i * 2 + target % 2, pl.ds(pl.multiple_of((target // 2) * 32, 32), 32), 0:512]
+        return d_sum[layer * 8 + target * 2 + i % 2, pl.ds(pl.multiple_of((i // 2) * 32, 32), 32), 512:1024]
+
+    def way(layer, side, step, source, target, first, forth):
+        here, at = (x, at_x) if side == 0 else (y, at_y)
+        device = at((here + (1 if forth else 3)) % 4)
+        part = pl.ds(first, 2)
+        lane = 0 if forth else 1
+        sem = relay_sem if step == 0 else first_sem
+        for k in range(2):
+            remote(
+                source[k].at[side, lane, part],
+                target[k].at[side, lane, part],
+                early_send.at[k if step == 0 else 2 + k],
+                sem.at[layer, side, k],
+                device,
+            ).start()
+
+    def begin_exchange(layer, side):
+        here = x if side == 0 else y
+        base = layer * 4
+
+        def far(i, c):
+            numbers, scales = coded(share(layer, side, (here + 2) % 4, i))
+            lane = i // 2
+            sf[side, lane, base + i], sfs[side, lane, base + i] = numbers, scales
+            return c
+
+        lax.fori_loop(0, 4, far, 0)
+        way(layer, side, 0, (sf, sfs), (rf, rfs), base, True)
+        way(layer, side, 0, (sf, sfs), (rf, rfs), base + 2, False)
+
+        def near(i, c):
+            sn[side, 0, base + 2 + i], sns[side, 0, base + 2 + i] = coded(share(layer, side, (here + 1) % 4, 2 + i))
+            sn[side, 1, base + i], sns[side, 1, base + i] = coded(share(layer, side, (here + 3) % 4, i))
+            return c
+
+        lax.fori_loop(0, 2, near, 0)
+        way(layer, side, 1, (sn, sns), (rn, rns), base + 2, True)
+        way(layer, side, 1, (sn, sns), (rn, rns), base, False)
+
+    def pass_on(layer, side):
+        here = x if side == 0 else y
+        base = layer * 4
+        take(rf.at[side, :, pl.ds(base, 2)], relay_sem.at[layer, side, 0])
+        take(rfs.at[side, :, pl.ds(base, 2)], relay_sem.at[layer, side, 1])
+
+        def add(i, c):
+            at = base + i
+            up = share(layer, side, (here + 1) % 4, i) + rf[side, 0, at].astype(F32) * rfs[side, 0, at]
+            sn[side, 0, at], sns[side, 0, at] = coded(up)
+            at = base + 2 + i
+            down = share(layer, side, (here + 3) % 4, 2 + i) + rf[side, 1, at].astype(F32) * rfs[side, 1, at]
+            sn[side, 1, at], sns[side, 1, at] = coded(down)
+            return c
+
+        lax.fori_loop(0, 2, add, 0)
+        way(layer, side, 2, (sn, sns), (rn, rns), base, True)
+        way(layer, side, 2, (sn, sns), (rn, rns), base + 2, False)
+
+    def product(layer, c, left, right):
+        cols = slice(c * 256, c * 256 + 256)
+        return dot(left.reshape(512, 256), right[layer, :, cols], 1, 0).reshape(8, 64, 256)
+
+    def own_product(layer):
+        for c in range(4):
+            d_sum[layer * 8 : layer * 8 + 8, :, c * 256 : c * 256 + 256] = product(
+                layer, c, at_own[layer, core], g_own
+            )
+
+    def add_product(layer, side):
+        for c in (2 * side, 2 * side + 1):
+            d_sum[layer * 8 : layer * 8 + 8, :, c * 256 : c * 256 + 256] += product(layer, c, at_in[layer], g_in)
+
+    core_a.wait_recv()
+    own_product(1)
+    core_g1.wait_recv()
+    add_product(1, 0)
+    begin_exchange(1, 0)
+    add_product(1, 1)
+    begin_exchange(1, 1)
+    own_product(0)
+    core_g0.wait_recv()
+    add_product(0, 0)
+    begin_exchange(0, 0)
+    pass_on(1, 0)
+    add_product(0, 1)
+    begin_exchange(0, 1)
+    pass_on(1, 1)
+    pass_on(0, 0)
+    pass_on(0, 1)
+
     for layer in (1, 0):
-        if layer == 0:
-            core_g0.wait()
-        part = pl.ds(layer * 4, 4)
-        blocks = pl.ds(layer * 8, 8)
         for side in range(2):
-            for c in (2 * side, 2 * side + 1):
-                cols = slice(c * 256, c * 256 + 256)
-                d = dot(at_own[layer, core].reshape(512, 256), g_own[layer, :, cols], 1, 0)
-                d = d + dot(at_in[layer].reshape(512, 256), g_in[layer, :, cols], 1, 0)
-                d_sum[blocks, :, cols] = d.reshape(8, 64, 256)
-
-            def code_left(b, c, layer=layer):
-                yy, xx = b // 2, b % 2
-                for hi in range(2):
-                    numbers, scales = coded(d_sum[layer * 8 + b, hi * 32 : hi * 32 + 32, 0:512])
-                    sa[hi * 2 + xx, layer * 4 + yy] = numbers
-                    sas[hi * 2 + xx, layer * 4 + yy] = scales
+            take(rn.at[side, :, pl.ds(layer * 4, 4)], first_sem.at[layer, side, 0])
+            take(rns.at[side, :, pl.ds(layer * 4, 4)], first_sem.at[layer, side, 1])
+
+            def add_up(i, c, layer=layer, side=side):
+                at = layer * 4 + i
+                total = share(layer, side, y if side else x, i)
+                for lane in range(2):
+                    total = total + rn[side, lane, at].astype(F32) * rns[side, lane, at]
+                if side == 0:
+                    a_sum[at] = total
+                    sa2[i, layer], sa2s[i, layer] = coded(total)
+                else:
+                    b_sum[at] = total
+                    sb2[i, layer], sb2s[i, layer] = coded(total)
                 return c
 
-            def code_right(b, c, layer=layer):
-                yy, xx = b // 2, b % 2
-                for hi in range(2):
-                    numbers, scales = coded(d_sum[layer * 8 + b, hi * 32 : hi * 32 + 32, 512:1024])
-                    sb[yy, layer * 4 + hi * 2 + xx] = numbers
-                    sbs[yy, layer * 4 + hi * 2 + xx] = scales
-                return c
-
-            lax.fori_loop(0, 8, code_right if side else code_left, 0)
-            copies = []
+            lax.fori_loop(0, 4, add_up, 0)
             for p in (2, 1, 3):
                 tx, ty = (x + p) % 4, (y + p) % 4
-                k = ((layer * 2 + side) * 3 + p - 1) * 2
-                if side == 0:
-                    copies += [
-                        remote(sa.at[tx, part], ra.at[p - 1, part], rsend.at[k], rrecv.at[k], at_x(tx)),
-                        remote(sas.at[tx, part], ras.at[p - 1, part], rsend.at[k + 1], rrecv.at[k + 1], at_x(tx)),
-                    ]
-                else:
-                    copies += [
-                        remote(sb.at[ty, part], rb.at[p - 1, part], rsend.at[k], rrecv.at[k], at_y(ty)),
-                        remote(sbs.at[ty, part], rbs.at[p - 1, part], rsend.at[k + 1], rrecv.at[k + 1], at_y(ty)),
-                    ]
-            for c in copies:
-                c.start()
-            firsts[layer, side] = copies
-
-    own_rows = pl.ds(pl.multiple_of(samp * 32, 32), 32)
-    seconds = []
-    for layer in (1, 0):
-        for side in range(2):
-            for c in firsts[layer, side]:
-                c.wait()
-
-            def add_left(rest, c, layer=layer):
-                i = layer * 4 + rest
-                left = d_sum[layer * 8 + rest * 2 + xlo, own_rows, 0:512]
-                for p in range(3):
-                    left = left + ra[p, i].astype(F32) * ras[p, i]
-                a_sum[i] = left
-                sa2[rest, layer], sa2s[rest, layer] = coded(left)
-                return c
-
-            def add_right(rest, c, layer=layer):
-                i = layer * 4 + rest
-                high = pl.ds(pl.multiple_of((rest // 2) * 32, 32), 32)
-                right = d_sum[layer * 8 + y * 2 + rest % 2, high, 512:1024]
-                for p in range(3):
-                    right = right + rb[p, i].astype(F32) * rbs[p, i]
-                b_sum[i] = right
-                sb2[rest, layer], sb2s[rest, layer] = coded(right)
-                return c
-
-            lax.fori_loop(0, 4, add_right if side else add_left, 0)
-            copies = []
-            for p in (2, 1, 3):
-                tx, ty = (x + p) % 4, (y + p) % 4
-                k = 24 + ((layer * 2 + side) * 3 + p - 1) * 2
-                if side == 0:
-                    copies += [
-                        remote(sa2.at[ty, layer], ra2.at[p - 1, layer], rsend.at[k], rrecv.at[k], at_y(ty)),
-                        remote(sa2s.at[ty, layer], ra2s.at[p - 1, layer], rsend.at[k + 1], rrecv.at[k + 1], at_y(ty)),
-                    ]
-                else:
-                    copies += [
-                        remote(sb2.at[tx, layer], rb2.at[p - 1, layer], rsend.at[k], rrecv.at[k], at_x(tx)),
-                        remote(sb2s.at[tx, layer], rb2s.at[p - 1, layer], rsend.at[k + 1], rrecv.at[k + 1], at_x(tx)),
-                    ]
-            for c in copies:
-                c.start()
-            seconds += copies
-    for c in seconds:
-        c.wait()
+                parts = (
+                    ((sa2, ra2, ty, at_y(ty)), (sa2s, ra2s, ty, at_y(ty)))
+                    if side == 0
+                    else ((sb2, rb2, tx, at_x(tx)), (sb2s, rb2s, tx, at_x(tx)))
+                )
+                for k, (source, target, t, device) in enumerate(parts):
+                    k = 2 * side + k
+                    remote(
+                        source.at[t, layer], target.at[p - 1, layer], second_sem.at[0, k], second_sem.at[1, k], device
+                    ).start()
+    for k, ref in enumerate((ra2, ra2s, rb2, rb2s)):
+        take(ref, second_sem.at[1, k])
 
     for layer in range(2):
         left = a_sum[layer * 4 + y]
@@ -486,24 +521,30 @@
             z_sum[t, 8 + 4 * layer : 12 + 4 * layer] = right[4 * t : 4 * t + 4]
     for t in range(8):
         sz[t], szs[t] = coded(z_sum[t])
-    copies = []
     for p in (4, 3, 5, 2, 6, 1, 7):
         t = (zpos + p) % 8
-        k = 48 + (p - 1) * 2
-        copies += [
-            remote(sz.at[t], rz.at[p - 1], rsend.at[k], rrecv.at[k], at_z(t)),
-            remote(szs.at[t], rzs.at[p - 1], rsend.at[k + 1], rrecv.at[k + 1], at_z(t)),
-        ]
-    for c in copies:
-        c.start()
-    for c in copies:
-        c.wait()
+        remote(sz.at[t], rz.at[p - 1], third_sem.at[0, 0], third_sem.at[1, 0], at_z(t)).start()
+        remote(szs.at[t], rzs.at[p - 1], third_sem.at[0, 1], third_sem.at[1, 1], at_z(t)).start()
+    take(rz, third_sem.at[1, 0])
+    take(rzs, third_sem.at[1, 1])
     total = z_sum[zpos]
     for p in range(7):
         total = total + rz[p].astype(F32) * rzs[p]
     for layer in range(2):
         grads_ref[layer, :, 0:512] = total[4 * layer : 4 * layer + 4]
         grads_ref[layer, :, 512:1024] = total[8 + 4 * layer : 12 + 4 * layer]
+    take(halo_out, halo_sem.at[0])
+    take(start_rows.at[pl.ds(0, PLANE - 1)], old_sem.at[0])
+    take(end_rows.at[pl.ds(0, PLANE - 1)], new_sem.at[0])
+    core_a.wait_send()
+    core_g1.wait_send()
+    core_g0.wait_send()
+    for k, ref in enumerate((sf.at[0], sfs.at[0], sn, sns)):
+        take(ref, early_send.at[k])
+    for k, ref in enumerate((ra2, ra2s, rb2, rb2s)):
+        take(ref, second_sem.at[0, k])
+    take(rz, third_sem.at[0, 0])
+    take(rzs, third_sem.at[0, 1])
     store_end.wait()
 
 
@@ -517,9 +558,18 @@
             jax.ShapeDtypeStruct((2048, 256), BF16),
             jax.ShapeDtypeStruct((2, 4, 1024), F32),
         ],
-        in_specs=[hbm, hbm] + [vmem] * 9 + [hbm],
+        in_specs=[hbm] * 12,
         out_specs=[hbm, vmem],
         scratch_shapes=[
+            pltpu.VMEM((8, 2048), F32),
+            pltpu.VMEM((8, 2048), F32),
+            pltpu.VMEM((8, 2048), jnp.int32),
+            pltpu.VMEM((1, 2048), jnp.int32),
+            pltpu.VMEM((1, 2048), jnp.int32),
+            pltpu.VMEM((1, 2048), F32),
+            pltpu.VMEM((1, 2048), F32),
+            pltpu.VMEM((1, 2048), F32),
+            pltpu.VMEM((1, 2048), jnp.int32),
             pltpu.VMEM((2048, 256), BF16),
             pltpu.VMEM((2048, 256), BF16),
             pltpu.VMEM((2, 1024, 1024), BF16),
@@ -545,14 +595,14 @@
             pltpu.VMEM((2, 256, 1024), BF16),
             pltpu.VMEM((2, 256, 1024), BF16),
             pltpu.VMEM((16, 64, 1024), F32),
-            pltpu.VMEM((4, 8, 32, 512), I16),
-            pltpu.VMEM((4, 8, 1, 512), F32),
-            pltpu.VMEM((3, 8, 32, 512), I16),
-            pltpu.VMEM((3, 8, 1, 512), F32),
-            pltpu.VMEM((4, 8, 32, 512), I16),
-            pltpu.VMEM((4, 8, 1, 512), F32),
-            pltpu.VMEM((3, 8, 32, 512), I16),
-            pltpu.VMEM((3, 8, 1, 512), F32),
+            pltpu.VMEM((2, 2, 8, 32, 512), I16),
+            pltpu.VMEM((2, 2, 8, 1, 512), F32),
+            pltpu.VMEM((2, 2, 8, 32, 512), I16),
+            pltpu.VMEM((2, 2, 8, 1, 512), F32),
+            pltpu.VMEM((2, 2, 8, 32, 512), I16),
+            pltpu.VMEM((2, 2, 8, 1, 512), F32),
+            pltpu.VMEM((2, 2, 8, 32, 512), I16),
+            pltpu.VMEM((2, 2, 8, 1, 512), F32),
             pltpu.VMEM((8, 32, 512), F32),
             pltpu.VMEM((8, 32, 512), F32),
             pltpu.VMEM((4, 2, 32, 512), I16),
@@ -568,17 +618,17 @@
             pltpu.VMEM((8, 1, 512), F32),
             pltpu.VMEM((7, 16, 512), I16),
             pltpu.VMEM((7, 1, 512), F32),
-            dma((8,)),
+            dma((15,)),
             dma((2,)),
             dma((2,)),
-            dma((PLANE,)),
-            dma((PLANE,)),
-            dma((PLANE,)),
-            dma((PLANE,)),
+            dma((2,)),
             dma((3,)),
             dma((3,)),
-            dma((62,)),
-            dma((62,)),
+            dma((2, 2, 2)),
+            dma((2, 2, 2)),
+            dma((4,)),
+            dma((2, 4)),
+            dma((2, 2)),
         ],
         compiler_params=pltpu.CompilerParams(
             collective_id=1, has_side_effects=True, vmem_limit_bytes=58 << 20

time: 73.7 us -> 68.7 us (0.932)
  Pallas kernels: 72.6 us -> 67.9 us
    pallas_call x1, Pallas kernels: 70.6 us -> 65.9 us  [whole(): pl.pallas_call(functools.partial(kernel, scale), out_shape=[jax.ShapeDtyp...]
where the time goes in v4:
time: 68.7 us; the launch traced here: 68.6 us
  Pallas kernels  67.9 us (99%)
    pallas_call x1, Pallas kernels, whole(): pl.pallas_call(functools.partial(kernel, scale), out_shape=[jax.ShapeDtyp...  65.9 us
    pallas_call x1, Pallas kernels, finish(): pl.pallas_call(finish_kernel, out_shape=[jax.ShapeDtypeStruct(end.shape,...  2 us

profile of v4, /device:TPU:2, one launch (start us, length us, event | category | flops | bytes accessed | tf_op | source)
XLA Modules:
  0.0 68.6 jit_solution(206772570388134426)
XLA Ops:
  0.6 65.9 %shard_map.131 = (bf16[2048,256]{1,0:T(8,128)(2,1)}, f32[2,4,1024]{2,1,0:T(4,128)}) custom-call(bf16[2048,256]{1,0:T(8,128)(2,1)} %head_hbm.1, bf16[2048,256]{1,0:T(8,128)(2,1)} %flow_hbm.1, f32[8,2048]{1,0:T(8,128)} %bitcast.9, f32[8,2048]{1,0:T(8,128)} %bitcast.10, s32[8,2048]{1,0:T(8,128)} %bitcast.11, s32[1,2048]{1,0:T(1,128)} %bitcast.12, ...), custom_call_target="tpu_custom_call" | custom-call | tf_op jit(solution)/shard_map/pallas_call | solution.py:555
  66.6 2.0 %shard_map.132 = (bf16[2048,256]{1,0:T(8,128)(2,1)}, f32[2,4,1024]{2,1,0:T(4,128)}) custom-call(bf16[2048,256]{1,0:T(8,128)(2,1)} %get-tuple-element.4.end_ref, f32[2,4,1024]{2,1,0:T(4,128)} %get-tuple-element.5.grads_ref), custom_call_target="tpu_custom_call" | custom-call | tf_op jit(solution)/shard_map/pallas_call | solution.py:656

commit v5 on v4

--- a/solution.py
+++ b/solution.py
@@ -314,10 +314,8 @@
     small = eye(128)
 
     def one_tile(i, c):
-        turn_y = i // 4
-        turn_y = jnp.where(turn_y < 2, 2 - turn_y, 6 - turn_y)
-        turn_y = jnp.where(i >= 12, 0, jnp.where(i >= 8, 3, turn_y))
-        tile = ((y + turn_y) % 4) * 4 + (xlo * 2 + core + i) % 4
+        turn_y = (2 + 3 * (i % 4)) % 4
+        tile = ((y + turn_y) % 4) * 4 + (xlo * 2 + core + 2 + i // 4 + i) % 4
         lanes = pl.ds(pl.multiple_of(tile * 128, 128), 128)
         heads[tile, 264:266, :] = halo_in[0, 0:2, lanes]
         flows[tile, 264:266, :] = halo_in[0, 2:4, lanes]
@@ -370,17 +368,19 @@
 
     take(end_rows.at[pl.ds(0, PLANE - 1)], new_sem.at[1])
     cut_windows(end_rows, begin, targets)
-    g_own[1] = ((out_val[...] - targets[...].astype(F32)) * scale).astype(BF16)
-    core_g1 = remote(g_own.at[1], g_in.at[1], csend.at[1], crecv.at[1], at_core)
-    core_g1.start()
-    for c in range(4):
-        cols = slice(c * 256, c * 256 + 256)
-        back = dot(g_own[1], weights[1, cols, :], 1, 1)
-        z = z_val[:, cols]
-        sigma = jax.nn.sigmoid(z)
-        g_own[0, :, cols] = (back * sigma * (1.0 + z * (1.0 - sigma))).astype(BF16)
-    core_g0 = remote(g_own.at[0], g_in.at[0], csend.at[2], crecv.at[2], at_core)
-    core_g0.start()
+
+    def to_core(layer, side):
+        half = pl.ds(side * 512, 512)
+        k = 1 + layer * 2 + side
+        copy = remote(g_own.at[layer, :, half], g_in.at[layer, :, half], csend.at[k], crecv.at[k], at_core)
+        copy.start()
+        return copy
+
+    core_g = {}
+    for side in range(2):
+        half = slice(side * 512, side * 512 + 512)
+        g_own[1, :, half] = ((out_val[:, half] - targets[:, half].astype(F32)) * scale).astype(BF16)
+        core_g[1, side] = to_core(1, side)
 
     def share(layer, side, target, i):
         if side == 0:
@@ -458,20 +458,30 @@
         for c in (2 * side, 2 * side + 1):
             d_sum[layer * 8 : layer * 8 + 8, :, c * 256 : c * 256 + 256] += product(layer, c, at_in[layer], g_in)
 
+    own_product(1)
     core_a.wait_recv()
-    own_product(1)
-    core_g1.wait_recv()
+    core_g[1, 0].wait_recv()
     add_product(1, 0)
     begin_exchange(1, 0)
+    core_g[1, 1].wait_recv()
     add_product(1, 1)
     begin_exchange(1, 1)
+    for c in range(4):
+        cols = slice(c * 256, c * 256 + 256)
+        back = dot(g_own[1], weights[1, cols, :], 1, 1)
+        z = z_val[:, cols]
+        sigma = jax.nn.sigmoid(z)
+        g_own[0, :, cols] = (back * sigma * (1.0 + z * (1.0 - sigma))).astype(BF16)
+        if c % 2:
+            core_g[0, c // 2] = to_core(0, c // 2)
     own_product(0)
-    core_g0.wait_recv()
+    core_g[0, 0].wait_recv()
     add_product(0, 0)
     begin_exchange(0, 0)
-    pass_on(1, 0)
+    core_g[0, 1].wait_recv()
     add_product(0, 1)
     begin_exchange(0, 1)
+    pass_on(1, 0)
     pass_on(1, 1)
     pass_on(0, 0)
     pass_on(0, 1)
@@ -537,8 +547,8 @@
     take(start_rows.at[pl.ds(0, PLANE - 1)], old_sem.at[0])
     take(end_rows.at[pl.ds(0, PLANE - 1)], new_sem.at[0])
     core_a.wait_send()
-    core_g1.wait_send()
-    core_g0.wait_send()
+    for c in core_g.values():
+        c.wait_send()
     for k, ref in enumerate((sf.at[0], sfs.at[0], sn, sns)):
         take(ref, early_send.at[k])
     for k, ref in enumerate((ra2, ra2s, rb2, rb2s)):
@@ -622,8 +632,8 @@
             dma((2,)),
             dma((2,)),
             dma((2,)),
-            dma((3,)),
-            dma((3,)),
+            dma((5,)),
+            dma((5,)),
             dma((2, 2, 2)),
             dma((2, 2, 2)),
             dma((4,)),

time: 68.7 us -> 66.4 us (0.967)
  Pallas kernels: 67.9 us -> 65.6 us
    pallas_call x1, Pallas kernels: 65.9 us -> 63.6 us  [whole(): pl.pallas_call(functools.partial(kernel, scale), out_shape=[jax.ShapeDtyp...]
where the time goes in v5:
time: 66.4 us; the launch traced here: 66.3 us
  Pallas kernels  65.6 us (99%)
    pallas_call x1, Pallas kernels, whole(): pl.pallas_call(functools.partial(kernel, scale), out_shape=[jax.ShapeDtyp...  63.6 us
    pallas_call x1, Pallas kernels, finish(): pl.pallas_call(finish_kernel, out_shape=[jax.ShapeDtypeStruct(end.shape,...  2 us

profile of v5, /device:TPU:2, one launch (start us, length us, event | category | flops | bytes accessed | tf_op | source)
XLA Modules:
  0.0 66.3 jit_solution(4330289942360083560)
XLA Ops:
  0.6 63.6 %shard_map.131 = (bf16[2048,256]{1,0:T(8,128)(2,1)}, f32[2,4,1024]{2,1,0:T(4,128)}) custom-call(bf16[2048,256]{1,0:T(8,128)(2,1)} %head_hbm.1, bf16[2048,256]{1,0:T(8,128)(2,1)} %flow_hbm.1, f32[8,2048]{1,0:T(8,128)} %bitcast.9, f32[8,2048]{1,0:T(8,128)} %bitcast.10, s32[8,2048]{1,0:T(8,128)} %bitcast.11, s32[1,2048]{1,0:T(1,128)} %bitcast.12, ...), custom_call_target="tpu_custom_call" | custom-call | tf_op jit(solution)/shard_map/pallas_call | solution.py:565
  64.3 2.0 %shard_map.132 = (bf16[2048,256]{1,0:T(8,128)(2,1)}, f32[2,4,1024]{2,1,0:T(4,128)}) custom-call(bf16[2048,256]{1,0:T(8,128)(2,1)} %get-tuple-element.4.end_ref, f32[2,4,1024]{2,1,0:T(4,128)} %get-tuple-element.5.grads_ref), custom_call_target="tpu_custom_call" | custom-call | tf_op jit(solution)/shard_map/pallas_call | solution.py:666

commit v6 on v5

--- a/solution.py
+++ b/solution.py
@@ -416,6 +416,10 @@
         way(layer, side, 0, (sf, sfs), (rf, rfs), base, True)
         way(layer, side, 0, (sf, sfs), (rf, rfs), base + 2, False)
 
+    def direct(layer, side):
+        here = x if side == 0 else y
+        base = layer * 4
+
         def near(i, c):
             sn[side, 0, base + 2 + i], sns[side, 0, base + 2 + i] = coded(share(layer, side, (here + 1) % 4, 2 + i))
             sn[side, 1, base + i], sns[side, 1, base + i] = coded(share(layer, side, (here + 3) % 4, i))
@@ -466,6 +470,8 @@
     core_g[1, 1].wait_recv()
     add_product(1, 1)
     begin_exchange(1, 1)
+    direct(1, 0)
+    direct(1, 1)
     for c in range(4):
         cols = slice(c * 256, c * 256 + 256)
         back = dot(g_own[1], weights[1, cols, :], 1, 1)
@@ -481,6 +487,8 @@
     core_g[0, 1].wait_recv()
     add_product(0, 1)
     begin_exchange(0, 1)
+    direct(0, 0)
+    direct(0, 1)
     pass_on(1, 0)
     pass_on(1, 1)
     pass_on(0, 0)

time: 66.4 us -> 65.8 us (level)
  no operation moved by 1% of the time
where the time goes in v6:
time: 65.8 us; the launch traced here: 65.7 us
  Pallas kernels  65.1 us (99%)
    pallas_call x1, Pallas kernels, whole(): pl.pallas_call(functools.partial(kernel, scale), out_shape=[jax.ShapeDtyp...  63.1 us
    pallas_call x1, Pallas kernels, finish(): pl.pallas_call(finish_kernel, out_shape=[jax.ShapeDtypeStruct(end.shape,...  2 us

profile of v6, /device:TPU:2, one launch (start us, length us, event | category | flops | bytes accessed | tf_op | source)
XLA Modules:
  0.0 65.7 jit_solution(6996765031545924257)
XLA Ops:
  0.6 63.1 %shard_map.131 = (bf16[2048,256]{1,0:T(8,128)(2,1)}, f32[2,4,1024]{2,1,0:T(4,128)}) custom-call(bf16[2048,256]{1,0:T(8,128)(2,1)} %head_hbm.1, bf16[2048,256]{1,0:T(8,128)(2,1)} %flow_hbm.1, f32[8,2048]{1,0:T(8,128)} %bitcast.9, f32[8,2048]{1,0:T(8,128)} %bitcast.10, s32[8,2048]{1,0:T(8,128)} %bitcast.11, s32[1,2048]{1,0:T(1,128)} %bitcast.12, ...), custom_call_target="tpu_custom_call" | custom-call | tf_op jit(solution)/shard_map/pallas_call | solution.py:573
  63.7 2.0 %shard_map.132 = (bf16[2048,256]{1,0:T(8,128)(2,1)}, f32[2,4,1024]{2,1,0:T(4,128)}) custom-call(bf16[2048,256]{1,0:T(8,128)(2,1)} %get-tuple-element.4.end_ref, f32[2,4,1024]{2,1,0:T(4,128)} %get-tuple-element.5.grads_ref), custom_call_target="tpu_custom_call" | custom-call | tf_op jit(solution)/shard_map/pallas_call | solution.py:674
